TPU v7x, 512 devices: a whole 4x4x16 slice. The times are simulated.
512 devices in a mesh: cell: 64 (over z, y_lo, core), inst: 8 (over x, y_hi).
Axes of the slice: x: 4, y: 4 (y_hi: 2, y_lo: 2; y = y_hi * 2 + y_lo), z: 16, core: 2. Of those that a mesh axis runs over, the one named last changes fastest.
Arguments:
- initial: float32 [80, 131072], P('inst', 'cell'), may hold values from -6 to 6
- source: float32 [80, 131072], P('inst', 'cell'), may hold values from -6 to 6
- neighbors: int32 [4, 131072], P(None, 'cell'), may hold values from -256 to 256, as said below
- face_weights: float32 [4, 131072], P(None, 'cell'), may hold values from 0.25 to 1
- damping: float32 [131072], P('cell'), may hold values from 0.5 to 2
Outputs:
- solution: float32 [80, 131072], P('inst', 'cell')
Inputs may be any that keep to these rules, and one draw needn't show every extreme that they name: `neighbors`: entries 0 and 2 of a cell's offsets are at or below zero, entries 1 and 3 at or above zero; a cell plus each of its offsets is a cell of the grid; in every draw some offsets are exactly -256 and exactly 256.
All inputs are finite; a program needn't handle non-finite values.
Results may differ from a plain program's by a relative error of at most 0.0001.
Values sent between devices are 32-bit elements; how exact they have to be, the bound alone decides.
A program may use at most 64 MiB of HBM per device.

v0:
```python
import jax
import jax.numpy as jnp
from jax import lax
from jax.sharding import PartitionSpec as P

NI = 16
NC = 4
COMP = 5
NEIGH = 4
SWEEPS_FINE = 2
SWEEPS_COARSE = 3
PLANE = 256


FREQ = 0.15
RELAX = 0.6


def padded_2(block, sides, width):
    for axis, dim in sides:
        count = lax.axis_size(axis)
        forward = [(i, i + 1) for i in range(count - 1)]
        backward = [(target, source) for source, target in forward]
        low = lax.ppermute(
            lax.slice_in_dim(block, block.shape[dim] - width, None, axis=dim), axis, forward
        )
        high = lax.ppermute(lax.slice_in_dim(block, 0, width, axis=dim), axis, backward)
        block = jnp.concatenate([low, block, high], axis=dim)
    return block


def spectral_matrix(points):
    steps = jnp.arange(points, dtype=jnp.float32)
    offset = steps[:, None] - steps[None, :]
    parity = 1.0 - 2.0 * jnp.mod(offset, 2.0)
    angle = jnp.where(offset == 0, 0.5, jnp.pi * offset / points)
    return jnp.where(offset == 0, 0.0, 0.5 * parity / jnp.tan(angle))


def restrict_matrix():
    coarse_t = jnp.arange(NC, dtype=jnp.float32) / NC
    fine_t = jnp.arange(NI, dtype=jnp.float32) / NI
    return (1.0 + 2.0 * jnp.cos(2.0 * jnp.pi * (coarse_t[:, None] - fine_t[None, :]))) / NI


def prolong_matrix():
    coarse_t = jnp.arange(NC, dtype=jnp.float32) / NC
    fine_t = jnp.arange(NI, dtype=jnp.float32) / NI
    return (1.0 + 2.0 * jnp.cos(2.0 * jnp.pi * (fine_t[:, None] - coarse_t[None, :]))) / NC


def expand(matrix):
    return jnp.kron(matrix, jnp.eye(COMP, dtype=jnp.float32))


def neighbour_terms(padded, flat_index, face_weights):
    cells = face_weights.shape[1]
    picked = jnp.take(padded, flat_index, axis=1).reshape(padded.shape[0], NEIGH, cells)
    return jnp.sum(face_weights[None, :, :] * picked, axis=1)


def fine_stencil(values, flat_index, face_weights):
    padded = padded_2(values, (("cell", 1),), PLANE)
    return neighbour_terms(padded, flat_index, face_weights)


def coarse_stencil(values, flat_index, face_weights):
    padded = padded_2(values, ((("cell", "inst"), 1),), PLANE)
    return neighbour_terms(padded, flat_index, face_weights)


def per_device(initial, source, neighbors, face_weights, damping):
    cells = initial.shape[1]
    own_count = initial.shape[0]
    inst_count = lax.axis_size("inst")
    inst_id = lax.axis_index("inst")
    highest = lax.Precision.HIGHEST
    fine_matrix = expand(spectral_matrix(NI))
    coarse_matrix = expand(spectral_matrix(NC))
    own_rows = lax.dynamic_slice_in_dim(fine_matrix, inst_id * own_count, own_count, 0)
    diagonal = damping + jnp.sum(face_weights, axis=0)
    position = jnp.arange(cells, dtype=jnp.int32)
    fine_index = (neighbors + position[None, :] + PLANE).reshape(-1)

    def derivative(values):
        gathered = lax.all_gather(values, "inst", axis=0, tiled=True)
        return jnp.dot(own_rows, gathered, precision=highest)

    def fine_operator(values):
        return (
            FREQ * derivative(values)
            + diagonal * values
            - fine_stencil(values, fine_index, face_weights)
        )

    solution = initial
    for sweep in range(SWEEPS_FINE):
        solution = solution + RELAX * (source - fine_operator(solution)) / diagonal
    residual = source - fine_operator(solution)
    own_columns = lax.dynamic_slice_in_dim(
        expand(restrict_matrix()), inst_id * own_count, own_count, 1
    )
    partial_terms = jnp.dot(own_columns, residual, precision=highest)
    prolong_rows = lax.dynamic_slice_in_dim(
        expand(prolong_matrix()), inst_id * own_count, own_count, 0
    )
    coarse_rhs = lax.psum_scatter(partial_terms, "inst", scatter_dimension=1, tiled=True)
    share = cells // inst_count
    share_weights = lax.dynamic_slice_in_dim(face_weights, inst_id * share, share, 1)
    share_diagonal = lax.dynamic_slice_in_dim(diagonal, inst_id * share, share, 0)
    share_offsets = lax.dynamic_slice_in_dim(neighbors, inst_id * share, share, 1)
    share_position = jnp.arange(share, dtype=jnp.int32)
    share_index = (share_offsets + share_position[None, :] + PLANE).reshape(-1)
    correction = RELAX * coarse_rhs / share_diagonal
    for sweep in range(SWEEPS_COARSE - 1):
        spectral = jnp.dot(coarse_matrix, correction, precision=highest)
        applied = (
            FREQ * spectral
            + share_diagonal * correction
            - coarse_stencil(correction, share_index, share_weights)
        )
        correction = correction + RELAX * (coarse_rhs - applied) / share_diagonal
    whole_correction = lax.all_gather(correction, "inst", axis=1, tiled=True)
    return solution + jnp.dot(prolong_rows, whole_correction, precision=highest)


def solution(mesh):
    return jax.shard_map(
        per_device,
        mesh=mesh,
        in_specs=(
            P("inst", "cell"),
            P("inst", "cell"),
            P(None, "cell"),
            P(None, "cell"),
            P("cell"),
        ),
        out_specs=P("inst", "cell"),
        check_vma=False,
    )
```

profile of v0, /device:TPU:128, one launch (start us, length us, event | category | flops | bytes accessed | tf_op | source)
XLA Modules:
  0.0 418.6 jit_solution(3546796274003178314)
XLA Ops:
  7.3 1.9 collective-permute-start
  9.2 5.8 %collective-permute-start.1 = (f32[10,256]{1,0:T(8,128)S(1)}, f32[10,256]{1,0:T(8,128)S(1)}, u32[]{:S(2)}, u32[]{:S(2)}) collective-permute-start(f32[10,256]{1,0:T(8,128)S(1)} %get-tuple-element.12), channel_id=1, source_target_pairs={{8,0},{16,8},{24,16},{32,24},{40,32},{48,40},{56,48},{64,56},{72,6... | collective-permute-start | bytes 30728 | tf_op jit(solution)/shard_map/ppermute | solution.py:27
  16.7 38.0 %all-gather = f32[8,10,2048]{2,1,0:T(8,128)S(1)} all-gather(f32[1,10,2048]{2,1,0:T(8,128)} %bitcast.47), channel_id=1, replica_groups=mesh['cell'=64,'inst'=8] {'inst'}, dimensions={0}, use_global_device_ids=true | all-gather | bytes 737280 | tf_op jit(solution)/shard_map/all_gather | solution.py:86
  56.2 27.8 %gather_fusion = f32[8192,10]{1,0:T(8,128)} fusion(f32[10,2560]{0,1:T(8,128)S(1)} %copy.21, s32[8192]{0:T(1024)S(1)} %fusion.27), kind=kCustom, calls=%fused_computation.clone | custom fusion | bytes 688128 | tf_op jit(solution)/shard_map/jit(_take)/gather | solution.py:58
  84.1 6.2 %broadcast_select_fusion.2 = f32[8192,10]{1,0:T(8,128)S(1)} fusion(f32[8192,10]{1,0:T(8,128)} %gather_fusion, pred[8192]{0:T(1024)(128)(4,1)S(1)} %compare_and_fusion), kind=kLoop, calls=%fused_computation.29 | loop fusion | flops 81920 | bytes 663552 | tf_op jit(solution)/shard_map/jit(_take)/select_n | solution.py:58
  90.3 1.6 multiply_reduce_fusion.2
  92.7 1.9 collective-permute-start.2
  94.6 5.8 %collective-permute-start.3 = (f32[10,256]{1,0:T(8,128)S(1)}, f32[10,256]{1,0:T(8,128)S(1)}, u32[]{:S(2)}, u32[]{:S(2)}) collective-permute-start(f32[10,256]{1,0:T(8,128)S(1)} %get-tuple-element.10), channel_id=1, source_target_pairs={{8,0},{16,8},{24,16},{32,24},{40,32},{48,40},{56,48},{64,56},{72,6... | collective-permute-start | bytes 30728 | tf_op jit(solution)/shard_map/ppermute | solution.py:27
  100.4 36.9 %all-gather.1 = f32[8,10,2048]{2,1,0:T(8,128)S(1)} all-gather(f32[1,10,2048]{2,1,0:T(8,128)S(1)} %bitcast.44), channel_id=1, replica_groups=mesh['cell'=64,'inst'=8] {'inst'}, dimensions={0}, use_global_device_ids=true | all-gather | bytes 737280 | tf_op jit(solution)/shard_map/all_gather | solution.py:86
  137.9 27.8 %gather_fusion.1 = f32[8192,10]{1,0:T(8,128)} fusion(f32[10,2560]{0,1:T(8,128)S(1)} %copy.23, s32[8192]{0:T(1024)S(1)} %fusion.27), kind=kCustom, calls=%fused_computation.2.clone | custom fusion | bytes 688128 | tf_op jit(solution)/shard_map/jit(_take)/gather | solution.py:58
  165.8 6.2 %broadcast_select_fusion.1 = f32[8192,10]{1,0:T(8,128)S(1)} fusion(f32[8192,10]{1,0:T(8,128)} %gather_fusion.1, pred[8192]{0:T(1024)(128)(4,1)S(1)} %compare_and_fusion), kind=kLoop, calls=%fused_computation.28 | loop fusion | flops 81920 | bytes 663552 | tf_op jit(solution)/shard_map/jit(_take)/select_n | solution.py:58
  172.0 1.6 multiply_reduce_fusion.1
  174.4 1.9 collective-permute-start.4
  176.3 5.8 %collective-permute-start.5 = (f32[10,256]{1,0:T(8,128)S(1)}, f32[10,256]{1,0:T(8,128)S(1)}, u32[]{:S(2)}, u32[]{:S(2)}) collective-permute-start(f32[10,256]{1,0:T(8,128)S(1)} %get-tuple-element.8), channel_id=1, source_target_pairs={{8,0},{16,8},{24,16},{32,24},{40,32},{48,40},{56,48},{64,56},{72,6... | collective-permute-start | bytes 30728 | tf_op jit(solution)/shard_map/ppermute | solution.py:27
  182.1 36.5 %all-gather.2 = f32[8,10,2048]{2,1,0:T(8,128)S(1)} all-gather(f32[1,10,2048]{2,1,0:T(8,128)S(1)} %bitcast.43), channel_id=1, replica_groups=mesh['cell'=64,'inst'=8] {'inst'}, dimensions={0}, use_global_device_ids=true | all-gather | bytes 737280 | tf_op jit(solution)/shard_map/all_gather | solution.py:86
  219.1 27.8 %gather_fusion.2 = f32[8192,10]{1,0:T(8,128)} fusion(f32[10,2560]{0,1:T(8,128)S(1)} %copy.26, s32[8192]{0:T(1024)S(1)} %fusion.27), kind=kCustom, calls=%fused_computation.3.clone | custom fusion | bytes 688128 | tf_op jit(solution)/shard_map/jit(_take)/gather | solution.py:58
  247.0 6.2 %broadcast_select_fusion = f32[8192,10]{1,0:T(8,128)S(1)} fusion(f32[8192,10]{1,0:T(8,128)} %gather_fusion.2, pred[8192]{0:T(1024)(128)(4,1)S(1)} %compare_and_fusion), kind=kLoop, calls=%fused_computation.27 | loop fusion | flops 81920 | bytes 663552 | tf_op jit(solution)/shard_map/jit(_take)/select_n | solution.py:58
  253.2 1.6 multiply_reduce_fusion
  255.5 1.0 fusion.28
  256.7 85.6 %reduce-scatter.2.cloned.1.call-done = f32[20,256]{1,0:T(8,128)} async-done(((f32[20,2048]{1,0:T(8,128)}), f32[20,256]{1,0:T(8,128)}) %reduce-scatter.2.cloned.1.call-update) | async-done | bytes 20496 | tf_op jit(solution)/shard_map/reduce_scatter | solution.py:107
  342.4 0.8 multiply_divide_fusion
  343.2 4.3 %collective-permute-start.6 = (f32[20,256]{1,0:T(8,128)S(1)}, f32[20,256]{1,0:T(8,128)S(1)}, u32[]{:S(2)}, u32[]{:S(2)}) collective-permute-start(f32[20,256]{1,0:T(8,128)S(1)} %multiply_divide_fusion), channel_id=1, source_target_pairs={{0,1},{1,2},{2,3},{3,4},{4,5},{5,6},{6,7},{7,8},{8,9},{9,10},{10,1... | collective-permute-start | bytes 61448 | tf_op jit(solution)/shard_map/ppermute | solution.py:24
  347.5 6.7 %collective-permute-start.7 = (f32[20,256]{1,0:T(8,128)S(1)}, f32[20,256]{1,0:T(8,128)S(1)}, u32[]{:S(2)}, u32[]{:S(2)}) collective-permute-start(f32[20,256]{1,0:T(8,128)S(1)} %multiply_divide_fusion), channel_id=1, source_target_pairs={{1,0},{2,1},{3,2},{4,3},{5,4},{6,5},{7,6},{8,7},{9,8},{10,9},{11,1... | collective-permute-start | bytes 61448 | tf_op jit(solution)/shard_map/ppermute | solution.py:27
  354.4 1.3 collective-permute-done.7
  355.9 2.8 gather_fusion.3
  359.2 1.0 fusion.26
  360.2 3.5 collective-permute-start.8
  363.7 7.4 %collective-permute-start.9 = (f32[20,256]{1,0:T(8,128)S(1)}, f32[20,256]{1,0:T(8,128)S(1)}, u32[]{:S(2)}, u32[]{:S(2)}) collective-permute-start(f32[20,256]{1,0:T(8,128)S(1)} %fusion.26), channel_id=1, source_target_pairs={{1,0},{2,1},{3,2},{4,3},{5,4},{6,5},{7,6},{8,7},{9,8},{10,9},{11,1... | collective-permute-start | bytes 61448 | tf_op jit(solution)/shard_map/ppermute | solution.py:27
  371.4 1.3 collective-permute-done.9
  372.9 2.8 gather_fusion.4
  376.4 34.3 %all_gather.15 = f32[20,2048]{1,0:T(8,128)S(1)} all-gather(f32[20,256]{1,0:T(8,128)S(1)} %fusion.20), channel_id=1, replica_groups=mesh['cell'=64,'inst'=8] {'inst'}, dimensions={1}, use_global_device_ids=true | all-gather | bytes 184320 | tf_op jit(solution)/shard_map/all_gather | solution.py:123
  410.7 1.1 convolution_add_fusion
  (77 shorter events, 9.4 us)
Async XLA Ops:
  6.5 49.2 %copy-start = (f32[10,2048]{1,0:T(8,128)S(1)}, f32[10,2048]{1,0:T(8,128)}, u32[]{:S(2)}) copy-start(f32[10,2048]{1,0:T(8,128)} %param.9) | copy-start | bytes 245764
  6.5 49.1 %copy-start.2 = (f32[4,2048]{1,0:T(4,128)S(1)}, f32[4,2048]{1,0:T(4,128)}, u32[]{:S(2)}) copy-start(f32[4,2048]{1,0:T(4,128)} %param.12) | copy-start | bytes 98308
  6.5 49.1 %copy-start.4 = (f32[2048]{0:T(1024)S(1)}, f32[2048]{0:T(1024)}, u32[]{:S(2)}) copy-start(f32[2048]{0:T(1024)} %param.13) | copy-start | bytes 24580
  6.5 335.8 %reduce-scatter.2.cloned.1.call-start = ((), (), s32[]{:S(2)}) async-start(), calls=%async_computation.1 | async-start | bytes 221184 | tf_op jit(solution)/shard_map/reduce_scatter | solution.py:107
  7.3 48.4 %collective-permute-start = (f32[10,256]{1,0:T(8,128)S(1)}, f32[10,256]{1,0:T(8,128)S(1)}, u32[]{:S(2)}, u32[]{:S(2)}) collective-permute-start(f32[10,256]{1,0:T(8,128)S(1)} %get-tuple-element.11), channel_id=1, source_target_pairs={{0,8},{8,16},{16,24},{24,32},{32,40},{40,48},{48,56},{56,64},{64,7... | collective-permute-start | bytes 30728 | tf_op jit(solution)/shard_map/ppermute | solution.py:24
  9.2 46.5 %collective-permute-start.1 = (f32[10,256]{1,0:T(8,128)S(1)}, f32[10,256]{1,0:T(8,128)S(1)}, u32[]{:S(2)}, u32[]{:S(2)}) collective-permute-start(f32[10,256]{1,0:T(8,128)S(1)} %get-tuple-element.12), channel_id=1, source_target_pairs={{8,0},{16,8},{24,16},{32,24},{40,32},{48,40},{56,48},{64,56},{72,6... | collective-permute-start | bytes 30728 | tf_op jit(solution)/shard_map/ppermute | solution.py:27
  90.3 1.9 copy-start.1
  92.7 44.7 %collective-permute-start.2 = (f32[10,256]{1,0:T(8,128)S(1)}, f32[10,256]{1,0:T(8,128)S(1)}, u32[]{:S(2)}, u32[]{:S(2)}) collective-permute-start(f32[10,256]{1,0:T(8,128)S(1)} %get-tuple-element.9), channel_id=1, source_target_pairs={{0,8},{8,16},{16,24},{24,32},{32,40},{40,48},{48,56},{56,64},{64,7... | collective-permute-start | bytes 30728 | tf_op jit(solution)/shard_map/ppermute | solution.py:24
  94.6 42.8 %collective-permute-start.3 = (f32[10,256]{1,0:T(8,128)S(1)}, f32[10,256]{1,0:T(8,128)S(1)}, u32[]{:S(2)}, u32[]{:S(2)}) collective-permute-start(f32[10,256]{1,0:T(8,128)S(1)} %get-tuple-element.10), channel_id=1, source_target_pairs={{8,0},{16,8},{24,16},{32,24},{40,32},{48,40},{56,48},{64,56},{72,6... | collective-permute-start | bytes 30728 | tf_op jit(solution)/shard_map/ppermute | solution.py:27
  174.4 44.3 %collective-permute-start.4 = (f32[10,256]{1,0:T(8,128)S(1)}, f32[10,256]{1,0:T(8,128)S(1)}, u32[]{:S(2)}, u32[]{:S(2)}) collective-permute-start(f32[10,256]{1,0:T(8,128)S(1)} %get-tuple-element.6), channel_id=1, source_target_pairs={{0,8},{8,16},{16,24},{24,32},{32,40},{40,48},{48,56},{56,64},{64,7... | collective-permute-start | bytes 30728 | tf_op jit(solution)/shard_map/ppermute | solution.py:24
  176.3 42.3 %collective-permute-start.5 = (f32[10,256]{1,0:T(8,128)S(1)}, f32[10,256]{1,0:T(8,128)S(1)}, u32[]{:S(2)}, u32[]{:S(2)}) collective-permute-start(f32[10,256]{1,0:T(8,128)S(1)} %get-tuple-element.8), channel_id=1, source_target_pairs={{8,0},{16,8},{24,16},{32,24},{40,32},{48,40},{56,48},{64,56},{72,6... | collective-permute-start | bytes 30728 | tf_op jit(solution)/shard_map/ppermute | solution.py:27
  342.4 33.8 %copy-start.3 = (f32[20,256]{1,0:T(8,128)S(1)}, f32[20,256]{1,0:T(8,128)}, u32[]{:S(2)}) copy-start(f32[20,256]{1,0:T(8,128)} %reduce-scatter.2.cloned.1.call-done) | copy-start | bytes 61444
  343.2 11.2 %collective-permute-start.6 = (f32[20,256]{1,0:T(8,128)S(1)}, f32[20,256]{1,0:T(8,128)S(1)}, u32[]{:S(2)}, u32[]{:S(2)}) collective-permute-start(f32[20,256]{1,0:T(8,128)S(1)} %multiply_divide_fusion), channel_id=1, source_target_pairs={{0,1},{1,2},{2,3},{3,4},{4,5},{5,6},{6,7},{7,8},{8,9},{9,10},{10,1... | collective-permute-start | bytes 61448 | tf_op jit(solution)/shard_map/ppermute | solution.py:24
  347.5 8.2 %collective-permute-start.7 = (f32[20,256]{1,0:T(8,128)S(1)}, f32[20,256]{1,0:T(8,128)S(1)}, u32[]{:S(2)}, u32[]{:S(2)}) collective-permute-start(f32[20,256]{1,0:T(8,128)S(1)} %multiply_divide_fusion), channel_id=1, source_target_pairs={{1,0},{2,1},{3,2},{4,3},{5,4},{6,5},{7,6},{8,7},{9,8},{10,9},{11,1... | collective-permute-start | bytes 61448 | tf_op jit(solution)/shard_map/ppermute | solution.py:27
  360.2 11.2 %collective-permute-start.8 = (f32[20,256]{1,0:T(8,128)S(1)}, f32[20,256]{1,0:T(8,128)S(1)}, u32[]{:S(2)}, u32[]{:S(2)}) collective-permute-start(f32[20,256]{1,0:T(8,128)S(1)} %fusion.26), channel_id=1, source_target_pairs={{0,1},{1,2},{2,3},{3,4},{4,5},{5,6},{6,7},{7,8},{8,9},{9,10},{10,1... | collective-permute-start | bytes 61448 | tf_op jit(solution)/shard_map/ppermute | solution.py:24
  363.7 8.9 %collective-permute-start.9 = (f32[20,256]{1,0:T(8,128)S(1)}, f32[20,256]{1,0:T(8,128)S(1)}, u32[]{:S(2)}, u32[]{:S(2)}) collective-permute-start(f32[20,256]{1,0:T(8,128)S(1)} %fusion.26), channel_id=1, source_target_pairs={{1,0},{2,1},{3,2},{4,3},{5,4},{6,5},{7,6},{8,7},{9,8},{10,9},{11,1... | collective-permute-start | bytes 61448 | tf_op jit(solution)/shard_map/ppermute | solution.py:27
Sparse Core Ops, SparseCore 0:
  256.7 85.5 reduce-scatter.1
where the time goes:
time: 419 us
  blocking collectives  146 us (35%)
  local copies, waits for them, and re-layouts  93.9 us (22%)
  waiting for transfers between devices  88.2 us (21%)
  starting transfers between devices  45 us (11%)
  other arithmetic  27.3 us (7%)
  between operations  13.9 us (3%)
  matrix products  4.6 us (1%)
    all_gather x3, blocking collectives, derivative(): gathered = lax.all_gather(values, 'inst', axis=0, tiled=True)  111 us
    gather x5, local copies, waits for them, and re-layouts, neighbour_terms(): jnp.take(padded, flat_index, axis=1).reshape(padded.shape[0], NEIGH, cells)  89.2 us
    reduce_scatter x1, waiting for transfers between devices, per_device(): lax.psum_scatter(partial_terms, 'inst', scatter_dimension=1, tiled=True)  85.6 us
    all_gather x1, blocking collectives, per_device(): whole_correction = lax.all_gather(correction, 'inst', axis=1, tiled=True)  34.3 us
    ppermute x5, starting transfers between devices, padded_2(): lax.ppermute(lax.slice_in_dim(block, 0, width, axis=dim), axis, backward)  31.4 us
    select_n x5, other arithmetic, neighbour_terms(): jnp.take(padded, flat_index, axis=1).reshape(padded.shape[0], NEIGH, cells)  19.1 us
    ppermute x5, starting transfers between devices, padded_2(): lax.ppermute(lax.slice_in_dim(block, block.shape[dim] - width, None, axis...  13.6 us
  transfers between devices with their start and end apart: 11, of which 3 were waited for; matrix products, arithmetic and copies ran while one was open for 1% of the time, Pallas kernels for 0%

commit v1 on v0

v1 whole, which is shorter than its diff:
```python
import math

import jax
import jax.numpy as jnp
from jax import lax
from jax.experimental import pallas as pl
from jax.experimental.pallas import tpu as pltpu
from jax.sharding import PartitionSpec as P

NI = 16
COMP = 5
NEIGH = 4
FREQ = 0.15
RELAX = 0.6
LANES = 128
OWN = 16
RIM = 4
WIDE = 8
ROWS = OWN + 2 * WIDE
GROUP = 8
PER = NI // GROUP
LOW = 3
MESH = pl.DeviceIdType.MESH
ROOT = math.sqrt(0.5)


def forward(x):
    out = [None] * NI
    p = [x[n] + x[n + 8] for n in range(8)]
    q = [x[n] - x[n + 8] for n in range(8)]
    q0, q4 = q[0] * 0.125, q[4] * 0.125
    d = [None] + [q[n] - q[8 - n] for n in (1, 2, 3)]
    s = [None] + [q[n] + q[8 - n] for n in (1, 2, 3)]
    for k in (1, 3, 5, 7):
        a, b = q0, (q4 if k in (1, 5) else -q4)
        for n in (1, 2, 3):
            a = a + d[n] * (math.cos(math.pi * k * n / 8) / 8)
            b = b + s[n] * (math.sin(math.pi * k * n / 8) / 8)
        out[2 * k - 1], out[2 * k] = a, b
    pp = [p[n] + p[n + 4] for n in range(4)]
    pq = [p[n] - p[n + 4] for n in range(4)]
    a, b = pq[0] * 0.125, pq[2] * 0.125
    d1, s1 = (pq[1] - pq[3]) * (ROOT / 8), (pq[1] + pq[3]) * (ROOT / 8)
    out[3], out[4] = a + d1, s1 + b
    out[11], out[12] = a - d1, s1 - b
    out[7], out[8] = (pp[0] - pp[2]) * 0.125, (pp[1] - pp[3]) * 0.125
    even, odd = (pp[0] + pp[2]) * 0.0625, (pp[1] + pp[3]) * 0.0625
    out[0], out[15] = even + odd, even - odd
    return out


def backward(h):
    a = {k: h[2 * k - 1] for k in range(1, 9)}
    a[0] = h[0]
    b = {k: h[2 * k] for k in range(1, 8)}
    odd = [None] * 8
    odd[0] = (a[1] + a[3]) + (a[5] + a[7])
    odd[4] = (b[1] - b[3]) + (b[5] - b[7])
    for n in (1, 2, 3):
        c = s = 0.0
        for k in (1, 3, 5, 7):
            c = c + a[k] * math.cos(math.pi * k * n / 8)
            s = s + b[k] * math.sin(math.pi * k * n / 8)
        odd[n], odd[8 - n] = s + c, s - c
    d, s = (a[2] - a[6]) * ROOT, (b[2] + b[6]) * ROOT
    half = [a[2] + a[6], s + d, b[2] - b[6], s - d]
    up, down = a[0] + a[8], a[0] - a[8]
    quarter = [up + a[4], down + b[4], up - a[4], down - b[4]]
    even = [quarter[n] + half[n] for n in range(4)] + [quarter[n] - half[n] for n in range(4)]
    return [even[n] + odd[n] for n in range(8)] + [even[n] - odd[n] for n in range(8)]


def owner(variable, cell):
    return variable + 3 * lax.rem(cell, 2)


def kernel(
    initial, source, neighbors, weights, damping, out,
    sx, sl, sr, stl, str_, ro, rl, rr, rstl, rstr,
    lane, step, gain, scale, u0, u1, src, low2, low3, low4, fin, back,
    s_own, s_left, s_right, s_stat, r_own, r_left, r_right, r_stat, s_low, r_low, s_out, r_out,
):
    cell, inst = lax.axis_index("cell"), lax.axis_index("inst")
    count = lax.axis_size("cell")
    after, before = lax.rem(cell + 1, count), lax.rem(cell + count - 1, count)
    mine = inst - 3 * lax.rem(cell, 2)
    busy = jnp.logical_and(mine >= 0, mine < COMP)

    def at(c, i):
        return {"cell": c, "inst": i}

    barrier = pltpu.get_barrier_semaphore()

    def greet(c, i):
        pl.semaphore_signal(barrier, inc=1, device_id=at(c, i), device_id_type=MESH)

    @pl.when(busy)
    def _():
        for j in range(1, GROUP):
            greet(cell, lax.rem(inst + j, GROUP))
        for c in (before, after):
            for i in range(GROUP):
                greet(c, i)

    @pl.when(jnp.logical_not(busy))
    def _():
        for v in range(COMP):
            greet(cell, owner(v, cell))

    for which, ref in enumerate((initial, source)):
        for n in range(PER):
            for v in range(COMP):
                x = ref[pl.ds(n * COMP + v, 1), :].reshape(OWN, LANES)
                sx[v, which, n] = x
                sl[v, which, n] = x[OWN - RIM :]
                sr[v, which, n] = x[:RIM]

    w = [weights[pl.ds(k, 1), :].reshape(OWN, LANES) for k in range(NEIGH)]
    off = [neighbors[pl.ds(k, 1), :].reshape(OWN, LANES) for k in range(NEIGH)]
    m = RELAX / (damping[...] + ((w[0] + w[1]) + (w[2] + w[3])))
    scale[WIDE : WIDE + OWN] = m
    stl[2 * NEIGH], str_[2 * NEIGH] = m[OWN - RIM :], m[:RIM]
    for k in range(NEIGH):
        g = w[k] * m
        position = lax.broadcasted_iota(jnp.int32, (OWN, LANES), 1) + off[k]
        lane[k, WIDE : WIDE + OWN] = position & (LANES - 1)
        step[k, WIDE : WIDE + OWN] = position >> 7
        gain[k, WIDE : WIDE + OWN] = g
        f = off[k].astype(jnp.float32)
        stl[k], str_[k] = f[OWN - RIM :], f[:RIM]
        stl[NEIGH + k], str_[NEIGH + k] = g[OWN - RIM :], g[:RIM]

    @pl.when(busy)
    def _():
        pl.semaphore_wait(barrier, 17)

    @pl.when(jnp.logical_not(busy))
    def _():
        pl.semaphore_wait(barrier, 15)

    def remote(a, b, s, r, c, i):
        return pltpu.make_async_remote_copy(
            src_ref=a, dst_ref=b, send_sem=s, recv_sem=r, device_id=at(c, i), device_id_type=MESH
        )

    own_copy = [
        remote(sx.at[v], ro.at[inst], s_own.at[v], r_own.at[inst], cell, owner(v, cell)) for v in range(COMP)
    ]
    left_copy = [
        remote(sl.at[v], rl.at[inst], s_left.at[v], r_left.at[inst], after, owner(v, after)) for v in range(COMP)
    ]
    right_copy = [
        remote(sr.at[v], rr.at[inst], s_right.at[v], r_right.at[inst], before, owner(v, before)) for v in range(COMP)
    ]
    for v in range(COMP):
        left_copy[v].start()
        right_copy[v].start()

        @pl.when(mine != v)
        def _():
            own_copy[v].start()

    @pl.when(busy)
    def _():
        stat = [
            remote(stl, rstl, s_stat.at[0], r_stat.at[0], after, owner(mine, after)),
            remote(str_, rstr, s_stat.at[1], r_stat.at[1], before, owner(mine, before)),
        ]
        keep = pltpu.make_async_copy(sx.at[mine], ro.at[inst], r_own.at[inst])
        keep.start()
        for copy in stat:
            copy.start()
        for copy in stat:
            copy.wait_recv()
        for start, got in ((WIDE - RIM, rstl), (WIDE + OWN, rstr)):
            rows = pl.ds(start, RIM)
            for k in range(NEIGH):
                position = lax.broadcasted_iota(jnp.int32, (RIM, LANES), 1) + got[k].astype(jnp.int32)
                lane[k, rows] = position & (LANES - 1)
                step[k, rows] = position >> 7
                gain[k, rows] = got[NEIGH + k]
            scale[rows] = got[2 * NEIGH]

        def arrived(ref, sem):
            for j in range(GROUP):
                pltpu.make_async_copy(ref.at[j], ref.at[j], sem.at[j]).wait()

        def transform(ref, first, rows, to):
            for which, dst in ((0, u0), (1, src)):
                h = forward([ref[n // PER, which, n % PER, pl.ds(first, rows)] for n in range(NI)])
                for j in range(NI):
                    dst[j, pl.ds(to, rows)] = h[j]

        arrived(rl, r_left)
        transform(rl, 0, RIM, WIDE - RIM)
        arrived(rr, r_right)
        transform(rr, 0, RIM, WIDE + OWN)
        arrived(ro, r_own)
        for t in range(OWN // 8):
            transform(ro, 8 * t, 8, WIDE + 8 * t)

        def sweep(old, new, start, to, harmonics):
            rows = pl.ds(start, 8)
            lanes = [lane[k, rows] for k in range(NEIGH)]
            steps = [step[k, rows] for k in range(NEIGH)]
            near = [steps[k] == 0 for k in range(NEIGH)]
            next_ = [steps[k] == (1 if k % 2 else -1) for k in range(NEIGH)]
            gains = [gain[k, rows] for k in range(NEIGH)]
            m = scale[rows]

            def coupled(j):
                x = {d: old[j, pl.ds(start + d, 8)] for d in (-2, -1, 0, 1, 2)}
                total = x[0] * (1.0 - RELAX)
                for k in range(NEIGH):
                    sign = 1 if k % 2 else -1
                    pick = [jnp.take_along_axis(x[sign * d], lanes[k], axis=1, mode="promise_in_bounds") for d in range(3)]
                    total = total + gains[k] * jnp.where(near[k], pick[0], jnp.where(next_[k], pick[1], pick[2]))
                return x[0], total

            for k in harmonics:
                if k in (0, 8):
                    j = max(2 * k - 1, 0)
                    _, total = coupled(j)
                    new[j, pl.ds(to, 8)] = total + m * src[j, rows]
                else:
                    a, b = 2 * k - 1, 2 * k
                    xa, ta = coupled(a)
                    xb, tb = coupled(b)
                    new[a, pl.ds(to, 8)] = ta + m * (src[a, rows] - (FREQ * k) * xb)
                    new[b, pl.ds(to, 8)] = tb + m * (src[b, rows] + (FREQ * k) * xa)

        low, high = (0, 1), tuple(range(2, 9))
        for start in (6, 14, 18):
            sweep(u0, u1, start, start, low)
        for start in (8, 16):
            sweep(u1, low2, start, start, low)
        wide = [
            remote(low2.at[:, pl.ds(OWN, WIDE)], low2.at[:, pl.ds(0, WIDE)], s_low.at[0], r_low.at[0], after, owner(mine, after)),
            remote(low2.at[:, pl.ds(WIDE, WIDE)], low2.at[:, pl.ds(WIDE + OWN, WIDE)], s_low.at[1], r_low.at[1], before, owner(mine, before)),
        ]
        for copy in wide:
            copy.start()
        for start in (6, 14, 18):
            sweep(u0, u1, start, start, high)
        for start in (8, 16):
            sweep(u1, fin, start, start - WIDE, high)
        for copy in wide:
            copy.wait_recv()
        for start in (4, 12, 20):
            sweep(low2, low3, start, start, low)
        for start in (6, 14, 18):
            sweep(low3, low4, start, start, low)
        for start in (8, 16):
            sweep(low4, fin, start, start - WIDE, low)
        for t in range(OWN // 8):
            rows = pl.ds(8 * t, 8)
            x = backward([fin[j, rows] for j in range(NI)])
            for n in range(NI):
                back[n // PER, n % PER, rows] = x[n]
        home = [
            remote(back.at[i], out.at[:, mine], s_out.at[i], r_out.at[mine], cell, i) for i in range(GROUP)
        ]
        for i in range(GROUP):

            @pl.when(inst != i)
            def _():
                home[i].start()

        stay = pltpu.make_async_copy(back.at[inst], out.at[:, mine], r_out.at[mine])
        stay.start()
        for i in range(GROUP):

            @pl.when(inst != i)
            def _():
                home[i].wait_send()

        for copy in wide + stat:
            copy.wait_send()

    for v in range(COMP):
        left_copy[v].wait_send()
        right_copy[v].wait_send()

        @pl.when(mine != v)
        def _():
            own_copy[v].wait_send()

    for v in range(COMP):
        pltpu.make_async_copy(out.at[:, v], out.at[:, v], r_out.at[v]).wait()


def per_device(initial, source, neighbors, face_weights, damping):
    vmem = pl.BlockSpec(memory_space=pltpu.VMEM)
    f32, i32 = jnp.float32, jnp.int32
    dma = pltpu.SemaphoreType.DMA
    tall = (NI, ROWS, LANES)
    low = (LOW, ROWS, LANES)
    result = pl.pallas_call(
        kernel,
        out_shape=jax.ShapeDtypeStruct((PER, COMP, OWN, LANES), f32),
        in_specs=[vmem] * 5,
        out_specs=vmem,
        scratch_shapes=[
            pltpu.VMEM((COMP, 2, PER, OWN, LANES), f32),
            pltpu.VMEM((COMP, 2, PER, RIM, LANES), f32),
            pltpu.VMEM((COMP, 2, PER, RIM, LANES), f32),
            pltpu.VMEM((2 * NEIGH + 1, RIM, LANES), f32),
            pltpu.VMEM((2 * NEIGH + 1, RIM, LANES), f32),
            pltpu.VMEM((GROUP, 2, PER, OWN, LANES), f32),
            pltpu.VMEM((GROUP, 2, PER, RIM, LANES), f32),
            pltpu.VMEM((GROUP, 2, PER, RIM, LANES), f32),
            pltpu.VMEM((2 * NEIGH + 1, RIM, LANES), f32),
            pltpu.VMEM((2 * NEIGH + 1, RIM, LANES), f32),
            pltpu.VMEM((NEIGH, ROWS, LANES), i32),
            pltpu.VMEM((NEIGH, ROWS, LANES), i32),
            pltpu.VMEM((NEIGH, ROWS, LANES), f32),
            pltpu.VMEM((ROWS, LANES), f32),
            pltpu.VMEM(tall, f32),
            pltpu.VMEM(tall, f32),
            pltpu.VMEM(tall, f32),
            pltpu.VMEM(low, f32),
            pltpu.VMEM(low, f32),
            pltpu.VMEM(low, f32),
            pltpu.VMEM((NI, OWN, LANES), f32),
            pltpu.VMEM((GROUP, PER, OWN, LANES), f32),
            dma((COMP,)), dma((COMP,)), dma((COMP,)), dma((2,)),
            dma((GROUP,)), dma((GROUP,)), dma((GROUP,)), dma((2,)),
            dma((2,)), dma((2,)), dma((GROUP,)), dma((COMP,)),
        ],
        compiler_params=pltpu.CompilerParams(
            collective_id=0, has_side_effects=True, vmem_limit_bytes=32 * 1024 * 1024
        ),
    )(initial, source, neighbors, face_weights, damping.reshape(OWN, LANES))
    return result.reshape(PER * COMP, OWN * LANES)


def solution(mesh):
    return jax.shard_map(
        per_device,
        mesh=mesh,
        in_specs=(
            P("inst", "cell"),
            P("inst", "cell"),
            P(None, "cell"),
            P(None, "cell"),
            P("cell"),
        ),
        out_specs=P("inst", "cell"),
        check_vma=False,
    )
```

time: 419 us -> 35.9 us (0.09)
  the two profiles are of different devices: /device:TPU:128 before, /device:TPU:4 now
where the time goes in v1:
time: 35.9 us; the launch traced here: 35.6 us
  Pallas kernels  30.9 us (86%)
  local copies, waits for them, and re-layouts  4.73 us (13%)
    pallas_call x1, Pallas kernels, per_device(): pl.pallas_call(kernel, out_shape=jax.ShapeDtypeStruct((PER, COMP, OWN, LA...  30.9 us
    unnamed x12, local copies, waits for them, and re-layouts  4.73 us

profile of v1, /device:TPU:4, one launch (start us, length us, event | category | flops | bytes accessed | tf_op | source)
XLA Modules:
  0.0 35.6 jit_solution(12863088575482194273)
XLA Ops:
  0.0 0.0 copy-start
  0.0 0.9 %copy-done = f32[10,2048]{1,0:T(8,128)S(1)} copy-done((f32[10,2048]{1,0:T(8,128)S(1)}, f32[10,2048]{1,0:T(8,128)}, u32[]{:S(2)}) %copy-start) | copy-done | bytes 81944
  0.9 0.0 copy-start.1
  0.9 0.9 %copy-done.1 = f32[10,2048]{1,0:T(8,128)S(1)} copy-done((f32[10,2048]{1,0:T(8,128)S(1)}, f32[10,2048]{1,0:T(8,128)}, u32[]{:S(2)}) %copy-start.1) | copy-done | bytes 81944
  1.8 0.0 copy-start.2
  1.8 0.8 %copy-done.2 = s32[4,2048]{1,0:T(4,128)S(1)} copy-done((s32[4,2048]{1,0:T(4,128)S(1)}, s32[4,2048]{1,0:T(4,128)}, u32[]{:S(2)}) %copy-start.2) | copy-done | bytes 32792
  2.6 0.0 copy-start.3
  2.6 0.8 %copy-done.3 = f32[4,2048]{1,0:T(4,128)S(1)} copy-done((f32[4,2048]{1,0:T(4,128)S(1)}, f32[4,2048]{1,0:T(4,128)}, u32[]{:S(2)}) %copy-start.3) | copy-done | bytes 32792
  3.3 0.0 copy-start.4
  3.3 0.7 %copy-done.4 = f32[2048]{0:T(1024)S(1)} copy-done((f32[2048]{0:T(1024)S(1)}, f32[2048]{0:T(1024)}, u32[]{:S(2)}) %copy-start.4) | copy-done | bytes 8216
  4.0 30.9 %shard_map.55 = f32[2,5,16,128]{3,2,1,0:T(8,128)S(1)} custom-call(f32[10,2048]{1,0:T(8,128)S(1)} %copy-done, f32[10,2048]{1,0:T(8,128)S(1)} %copy-done.1, s32[4,2048]{1,0:T(4,128)S(1)} %copy-done.2, f32[4,2048]{1,0:T(4,128)S(1)} %copy-done.3, f32[16,128]{1,0:T(8,128)S(1)} %bitcast.6), custom_call_target="tpu_custom_call" | custom-call | tf_op jit(solution)/shard_map/pallas_call | solution.py:298
  34.9 0.7 %copy.6 = f32[2,8,16,128]{3,1,2,0:T(8,128)} copy(f32[2,8,16,128]{3,2,1,0:T(8,128)S(1)} %bitcast.7) | data formatting | bytes 262144
  (1 shorter events, 0.0 us)
Async XLA Ops:
  0.0 0.9 %copy-start = (f32[10,2048]{1,0:T(8,128)S(1)}, f32[10,2048]{1,0:T(8,128)}, u32[]{:S(2)}) copy-start(f32[10,2048]{1,0:T(8,128)} %initial.1) | copy-start | bytes 245764
  0.9 0.9 %copy-start.1 = (f32[10,2048]{1,0:T(8,128)S(1)}, f32[10,2048]{1,0:T(8,128)}, u32[]{:S(2)}) copy-start(f32[10,2048]{1,0:T(8,128)} %source.1) | copy-start | bytes 245764
  1.8 0.8 %copy-start.2 = (s32[4,2048]{1,0:T(4,128)S(1)}, s32[4,2048]{1,0:T(4,128)}, u32[]{:S(2)}) copy-start(s32[4,2048]{1,0:T(4,128)} %neighbors.1) | copy-start | bytes 98308
  2.6 0.8 %copy-start.3 = (f32[4,2048]{1,0:T(4,128)S(1)}, f32[4,2048]{1,0:T(4,128)}, u32[]{:S(2)}) copy-start(f32[4,2048]{1,0:T(4,128)} %weights.1) | copy-start | bytes 98308
  3.3 0.7 %copy-start.4 = (f32[2048]{0:T(1024)S(1)}, f32[2048]{0:T(1024)}, u32[]{:S(2)}) copy-start(f32[2048]{0:T(1024)} %param.9) | copy-start | bytes 24580

commit v2 on v1

--- a/solution.py
+++ b/solution.py
@@ -75,20 +75,39 @@
 
 
 def kernel(
-    initial, source, neighbors, weights, damping, out,
+    initial_in, source_in, neighbors_in, weights_in, damping_in, out,
+    initial, source, neighbors, weights, damping,
     sx, sl, sr, stl, str_, ro, rl, rr, rstl, rstr,
     lane, step, gain, scale, u0, u1, src, low2, low3, low4, fin, back,
-    s_own, s_left, s_right, s_stat, r_own, r_left, r_right, r_stat, s_low, r_low, s_out, r_out,
+    s_in, s_own, s_left, s_right, s_stat, r_own, r_left, r_right, r_stat, s_low, r_low, s_out, r_out,
 ):
     cell, inst = lax.axis_index("cell"), lax.axis_index("inst")
     count = lax.axis_size("cell")
-    after, before = lax.rem(cell + 1, count), lax.rem(cell + count - 1, count)
+    first, last = cell == 0, cell == count - 1
+    has_before, has_after = jnp.logical_not(first), jnp.logical_not(last)
+    after, before = jnp.minimum(cell + 1, count - 1), jnp.maximum(cell - 1, 0)
+    sides = has_before.astype(jnp.int32) + has_after.astype(jnp.int32)
     mine = inst - 3 * lax.rem(cell, 2)
     busy = jnp.logical_and(mine >= 0, mine < COMP)
 
     def at(c, i):
         return {"cell": c, "inst": i}
 
+    load = [
+        pltpu.make_async_copy(a, b, s_in.at[j])
+        for j, (a, b) in enumerate(
+            (
+                (initial_in, initial),
+                (source_in, source),
+                (neighbors_in, neighbors),
+                (weights_in, weights),
+                (damping_in, damping),
+            )
+        )
+    ]
+    for copy in load:
+        copy.start()
+
     barrier = pltpu.get_barrier_semaphore()
 
     def greet(c, i):
@@ -98,9 +117,12 @@
     def _():
         for j in range(1, GROUP):
             greet(cell, lax.rem(inst + j, GROUP))
-        for c in (before, after):
-            for i in range(GROUP):
-                greet(c, i)
+        for has, c in ((has_before, before), (has_after, after)):
+
+            @pl.when(has)
+            def _():
+                for i in range(GROUP):
+                    greet(c, i)
 
     @pl.when(jnp.logical_not(busy))
     def _():
@@ -108,6 +130,7 @@
             greet(cell, owner(v, cell))
 
     for which, ref in enumerate((initial, source)):
+        load[which].wait()
         for n in range(PER):
             for v in range(COMP):
                 x = ref[pl.ds(n * COMP + v, 1), :].reshape(OWN, LANES)
@@ -115,6 +138,8 @@
                 sl[v, which, n] = x[OWN - RIM :]
                 sr[v, which, n] = x[:RIM]
 
+    for copy in load[2:]:
+        copy.wait()
     w = [weights[pl.ds(k, 1), :].reshape(OWN, LANES) for k in range(NEIGH)]
     off = [neighbors[pl.ds(k, 1), :].reshape(OWN, LANES) for k in range(NEIGH)]
     m = RELAX / (damping[...] + ((w[0] + w[1]) + (w[2] + w[3])))
@@ -132,11 +157,11 @@
 
     @pl.when(busy)
     def _():
-        pl.semaphore_wait(barrier, 17)
+        pl.semaphore_wait(barrier, GROUP - 1 + COMP * sides)
 
     @pl.when(jnp.logical_not(busy))
     def _():
-        pl.semaphore_wait(barrier, 15)
+        pl.semaphore_wait(barrier, COMP + COMP * sides)
 
     def remote(a, b, s, r, c, i):
         return pltpu.make_async_remote_copy(
@@ -152,9 +177,17 @@
     right_copy = [
         remote(sr.at[v], rr.at[inst], s_right.at[v], r_right.at[inst], before, owner(v, before)) for v in range(COMP)
     ]
+    @pl.when(has_after)
+    def _():
+        for v in range(COMP):
+            left_copy[v].start()
+
+    @pl.when(has_before)
+    def _():
+        for v in range(COMP):
+            right_copy[v].start()
+
     for v in range(COMP):
-        left_copy[v].start()
-        right_copy[v].start()
 
         @pl.when(mine != v)
         def _():
@@ -168,10 +201,41 @@
         ]
         keep = pltpu.make_async_copy(sx.at[mine], ro.at[inst], r_own.at[inst])
         keep.start()
-        for copy in stat:
-            copy.start()
-        for copy in stat:
-            copy.wait_recv()
+
+        @pl.when(has_after)
+        def _():
+            stat[0].start()
+
+        @pl.when(has_before)
+        def _():
+            stat[1].start()
+
+        def arrived(ref, sem):
+            for j in range(GROUP):
+                pltpu.make_async_copy(ref.at[j], ref.at[j], sem.at[j]).wait()
+
+        @pl.when(has_before)
+        def _():
+            stat[0].wait_recv()
+            arrived(rl, r_left)
+
+        @pl.when(first)
+        def _():
+            rl[...] = jnp.zeros_like(rl)
+            rstl[...] = jnp.zeros_like(rstl)
+            low2[:, :WIDE] = jnp.zeros((LOW, WIDE, LANES), jnp.float32)
+
+        @pl.when(has_after)
+        def _():
+            stat[1].wait_recv()
+            arrived(rr, r_right)
+
+        @pl.when(last)
+        def _():
+            rr[...] = jnp.zeros_like(rr)
+            rstr[...] = jnp.zeros_like(rstr)
+            low2[:, WIDE + OWN :] = jnp.zeros((LOW, WIDE, LANES), jnp.float32)
+
         for start, got in ((WIDE - RIM, rstl), (WIDE + OWN, rstr)):
             rows = pl.ds(start, RIM)
             for k in range(NEIGH):
@@ -181,19 +245,13 @@
                 gain[k, rows] = got[NEIGH + k]
             scale[rows] = got[2 * NEIGH]
 
-        def arrived(ref, sem):
-            for j in range(GROUP):
-                pltpu.make_async_copy(ref.at[j], ref.at[j], sem.at[j]).wait()
-
         def transform(ref, first, rows, to):
             for which, dst in ((0, u0), (1, src)):
                 h = forward([ref[n // PER, which, n % PER, pl.ds(first, rows)] for n in range(NI)])
                 for j in range(NI):
                     dst[j, pl.ds(to, rows)] = h[j]
 
-        arrived(rl, r_left)
         transform(rl, 0, RIM, WIDE - RIM)
-        arrived(rr, r_right)
         transform(rr, 0, RIM, WIDE + OWN)
         arrived(ro, r_own)
         for t in range(OWN // 8):
@@ -238,14 +296,28 @@
             remote(low2.at[:, pl.ds(OWN, WIDE)], low2.at[:, pl.ds(0, WIDE)], s_low.at[0], r_low.at[0], after, owner(mine, after)),
             remote(low2.at[:, pl.ds(WIDE, WIDE)], low2.at[:, pl.ds(WIDE + OWN, WIDE)], s_low.at[1], r_low.at[1], before, owner(mine, before)),
         ]
-        for copy in wide:
-            copy.start()
+
+        @pl.when(has_after)
+        def _():
+            wide[0].start()
+
+        @pl.when(has_before)
+        def _():
+            wide[1].start()
+
         for start in (6, 14, 18):
             sweep(u0, u1, start, start, high)
         for start in (8, 16):
             sweep(u1, fin, start, start - WIDE, high)
-        for copy in wide:
-            copy.wait_recv()
+
+        @pl.when(has_before)
+        def _():
+            wide[0].wait_recv()
+
+        @pl.when(has_after)
+        def _():
+            wide[1].wait_recv()
+
         for start in (4, 12, 20):
             sweep(low2, low3, start, start, low)
         for start in (6, 14, 18):
@@ -274,12 +346,27 @@
             def _():
                 home[i].wait_send()
 
-        for copy in wide + stat:
-            copy.wait_send()
+        @pl.when(has_after)
+        def _():
+            wide[0].wait_send()
+            stat[0].wait_send()
+
+        @pl.when(has_before)
+        def _():
+            wide[1].wait_send()
+            stat[1].wait_send()
+
+    @pl.when(has_after)
+    def _():
+        for v in range(COMP):
+            left_copy[v].wait_send()
+
+    @pl.when(has_before)
+    def _():
+        for v in range(COMP):
+            right_copy[v].wait_send()
 
     for v in range(COMP):
-        left_copy[v].wait_send()
-        right_copy[v].wait_send()
 
         @pl.when(mine != v)
         def _():
@@ -298,9 +385,14 @@
     result = pl.pallas_call(
         kernel,
         out_shape=jax.ShapeDtypeStruct((PER, COMP, OWN, LANES), f32),
-        in_specs=[vmem] * 5,
+        in_specs=[pl.BlockSpec(memory_space=pltpu.HBM)] * 5,
         out_specs=vmem,
         scratch_shapes=[
+            pltpu.VMEM((PER * COMP, OWN * LANES), f32),
+            pltpu.VMEM((PER * COMP, OWN * LANES), f32),
+            pltpu.VMEM((NEIGH, OWN * LANES), i32),
+            pltpu.VMEM((NEIGH, OWN * LANES), f32),
+            pltpu.VMEM((OWN, LANES), f32),
             pltpu.VMEM((COMP, 2, PER, OWN, LANES), f32),
             pltpu.VMEM((COMP, 2, PER, RIM, LANES), f32),
             pltpu.VMEM((COMP, 2, PER, RIM, LANES), f32),
@@ -323,12 +415,12 @@
             pltpu.VMEM(low, f32),
             pltpu.VMEM((NI, OWN, LANES), f32),
             pltpu.VMEM((GROUP, PER, OWN, LANES), f32),
-            dma((COMP,)), dma((COMP,)), dma((COMP,)), dma((2,)),
+            dma((5,)), dma((COMP,)), dma((COMP,)), dma((COMP,)), dma((2,)),
             dma((GROUP,)), dma((GROUP,)), dma((GROUP,)), dma((2,)),
             dma((2,)), dma((2,)), dma((GROUP,)), dma((COMP,)),
         ],
         compiler_params=pltpu.CompilerParams(
-            collective_id=0, has_side_effects=True, vmem_limit_bytes=32 * 1024 * 1024
+            collective_id=0, has_side_effects=True, vmem_limit_bytes=56 * 1024 * 1024
         ),
     )(initial, source, neighbors, face_weights, damping.reshape(OWN, LANES))
     return result.reshape(PER * COMP, OWN * LANES)

time: 35.9 us -> 28.5 us (0.79)
  the two profiles are of different devices: /device:TPU:4 before, /device:TPU:1 now
where the time goes in v2:
time: 28.5 us; the launch traced here: 28.3 us
  Pallas kernels  26.7 us (94%)
  local copies, waits for them, and re-layouts  1.6 us (6%)
    pallas_call x1, Pallas kernels, per_device(): pl.pallas_call(kernel, out_shape=jax.ShapeDtypeStruct((PER, COMP, OWN, LA...  26.7 us
    unnamed x2, local copies, waits for them, and re-layouts  1.6 us

profile of v2, /device:TPU:1, one launch (start us, length us, event | category | flops | bytes accessed | tf_op | source)
XLA Modules:
  0.0 28.3 jit_solution(9066177862214514615)
XLA Ops:
  0.0 26.7 %shard_map.55 = f32[2,5,16,128]{3,2,1,0:T(8,128)} custom-call(f32[10,2048]{1,0:T(8,128)} %initial_in.1, f32[10,2048]{1,0:T(8,128)} %source_in.1, s32[4,2048]{1,0:T(4,128)} %neighbors_in.1, f32[4,2048]{1,0:T(4,128)} %weights_in.1, f32[16,128]{1,0:T(8,128)} %bitcast.7), custom_call_target="tpu_custom_call" | custom-call | tf_op jit(solution)/shard_map/pallas_call | solution.py:385
  26.7 0.9 %pad = f32[16,16,128]{2,1,0:T(8,128)S(1)} pad(f32[10,16,128]{2,1,0:T(8,128)} %bitcast.6, f32[]{:T(128)} %constant.2), padding=0_6x0_0x0_0 | pad | bytes 212996
  27.6 0.7 %copy.6 = f32[2,8,16,128]{3,1,2,0:T(8,128)} copy(f32[2,8,16,128]{3,2,1,0:T(8,128)S(1)} %bitcast.5) | data formatting | bytes 262144

commit v3 on v2

v3 whole, which is shorter than its diff:
```python
import math

import jax
import jax.numpy as jnp
from jax import lax
from jax.experimental import pallas as pl
from jax.experimental.pallas import tpu as pltpu
from jax.sharding import PartitionSpec as P

NI = 16
COMP = 5
NEIGH = 4
FREQ = 0.15
RELAX = 0.6
LANES = 128
OWN = 16
SWEEPS_FINE = 2
SWEEPS = 5
REACH = 2
RIM = SWEEPS * REACH
RIM_S = RIM - REACH
ROWS = OWN + 2 * RIM
GROUP = 8
PER = NI // GROUP
MESSAGE = PER * (RIM + RIM_S) + 4
OWNERS = (0, 1, 2, 4, 6)
MESH = pl.DeviceIdType.MESH
ROOT = math.sqrt(0.5)


def forward(x):
    out = [None] * NI
    p = [x[n] + x[n + 8] for n in range(8)]
    q = [x[n] - x[n + 8] for n in range(8)]
    q0, q4 = q[0] * 0.125, q[4] * 0.125
    d = [None] + [q[n] - q[8 - n] for n in (1, 2, 3)]
    s = [None] + [q[n] + q[8 - n] for n in (1, 2, 3)]
    for k in (1, 3, 5, 7):
        a, b = q0, (q4 if k in (1, 5) else -q4)
        for n in (1, 2, 3):
            a = a + d[n] * (math.cos(math.pi * k * n / 8) / 8)
            b = b + s[n] * (math.sin(math.pi * k * n / 8) / 8)
        out[2 * k - 1], out[2 * k] = a, b
    pp = [p[n] + p[n + 4] for n in range(4)]
    pq = [p[n] - p[n + 4] for n in range(4)]
    a, b = pq[0] * 0.125, pq[2] * 0.125
    d1, s1 = (pq[1] - pq[3]) * (ROOT / 8), (pq[1] + pq[3]) * (ROOT / 8)
    out[3], out[4] = a + d1, s1 + b
    out[11], out[12] = a - d1, s1 - b
    out[7], out[8] = (pp[0] - pp[2]) * 0.125, (pp[1] - pp[3]) * 0.125
    even, odd = (pp[0] + pp[2]) * 0.0625, (pp[1] + pp[3]) * 0.0625
    out[0], out[15] = even + odd, even - odd
    return out


def backward(h):
    a = {k: h[2 * k - 1] for k in range(1, 9)}
    a[0] = h[0]
    b = {k: h[2 * k] for k in range(1, 8)}
    odd = [None] * 8
    odd[0] = (a[1] + a[3]) + (a[5] + a[7])
    odd[4] = (b[1] - b[3]) + (b[5] - b[7])
    for n in (1, 2, 3):
        c = s = 0.0
        for k in (1, 3, 5, 7):
            c = c + a[k] * math.cos(math.pi * k * n / 8)
            s = s + b[k] * math.sin(math.pi * k * n / 8)
        odd[n], odd[8 - n] = s + c, s - c
    d, s = (a[2] - a[6]) * ROOT, (b[2] + b[6]) * ROOT
    half = [a[2] + a[6], s + d, b[2] - b[6], s - d]
    up, down = a[0] + a[8], a[0] - a[8]
    quarter = [up + a[4], down + b[4], up - a[4], down - b[4]]
    even = [quarter[n] + half[n] for n in range(4)] + [quarter[n] - half[n] for n in range(4)]
    return [even[n] + odd[n] for n in range(8)] + [even[n] - odd[n] for n in range(8)]


def tiles(start, stop):
    return [min(row, stop - 8) for row in range(start, stop, 8)]


def kernel(
    initial_in, source_in, neighbors_in, weights_in, damping_in, out,
    initial, source, neighbors, weights, damping,
    sx, sl, sr, stl, str_, ro, rl, rr, rstl, rstr,
    lane, step, gain, scale, even, odd, src, fin, back,
    s_in, s_own, s_left, s_right, s_stat, r_own, r_left, r_right, r_stat, s_out, r_out,
):
    cell, inst = lax.axis_index("cell"), lax.axis_index("inst")
    count = lax.axis_size("cell")
    first, last = cell == 0, cell == count - 1
    has_before, has_after = jnp.logical_not(first), jnp.logical_not(last)
    after, before = jnp.minimum(cell + 1, count - 1), jnp.maximum(cell - 1, 0)
    sides = has_before.astype(jnp.int32) + has_after.astype(jnp.int32)
    mine, owns = 0, 0
    for v in range(COMP):
        here = (inst == OWNERS[v]).astype(jnp.int32)
        mine, owns = mine + v * here, owns + here
    busy = owns == 1
    idle = jnp.logical_not(busy)

    load = [
        pltpu.make_async_copy(a, b, s_in.at[j])
        for j, (a, b) in enumerate(
            (
                (initial_in, initial),
                (source_in, source),
                (neighbors_in, neighbors),
                (weights_in, weights),
                (damping_in, damping),
            )
        )
    ]
    for copy in load:
        copy.start()

    barrier = pltpu.get_barrier_semaphore()

    def greet(c, i):
        pl.semaphore_signal(barrier, inc=1, device_id={"cell": c, "inst": i}, device_id_type=MESH)

    @pl.when(busy)
    def _():
        for has, c in ((has_before, before), (has_after, after)):

            @pl.when(has)
            def _():
                for i in range(GROUP):
                    greet(c, i)

        for j in range(1, GROUP):
            greet(cell, lax.rem(inst + j, GROUP))

    for which, ref in enumerate((initial, source)):
        load[which].wait()
        for n in range(PER):
            for v in range(COMP):
                x = ref[pl.ds(n * COMP + v, 1), :].reshape(OWN, LANES)
                sx[v, which, n] = x
                size = (RIM, RIM_S)[which]
                rows = pl.ds((n * RIM, PER * RIM + n * RIM_S)[which], size)
                sl[v, rows] = x[OWN - size :]
                sr[v, rows] = x[:size]

    pl.semaphore_wait(barrier, COMP * (1 + sides) - owns)

    def remote(a, b, s, r, c, i):
        return pltpu.make_async_remote_copy(
            src_ref=a, dst_ref=b, send_sem=s, recv_sem=r, device_id={"cell": c, "inst": i}, device_id_type=MESH
        )

    own_copy = [remote(sx.at[v], ro.at[inst], s_own, r_own, cell, OWNERS[v]) for v in range(COMP)]
    left_copy = [remote(sl.at[v], rl.at[inst], s_left, r_left, after, OWNERS[v]) for v in range(COMP)]
    right_copy = [remote(sr.at[v], rr.at[inst], s_right, r_right, before, OWNERS[v]) for v in range(COMP)]

    for v in range(COMP):

        @pl.when(mine + COMP * (1 - owns) != v)
        def _():
            own_copy[v].start()

    @pl.when(has_after)
    def _():
        for v in range(COMP):
            left_copy[v].start()

    @pl.when(has_before)
    def _():
        for v in range(COMP):
            right_copy[v].start()

    @pl.when(busy)
    def _():
        for copy in load[2:]:
            copy.wait()
        w = [weights[pl.ds(k, 1), :].reshape(OWN, LANES) for k in range(NEIGH)]
        off = [neighbors[pl.ds(k, 1), :].reshape(OWN, LANES) for k in range(NEIGH)]
        m = RELAX / (damping[...] + ((w[0] + w[1]) + (w[2] + w[3])))
        own = pl.ds(RIM, OWN)
        scale[own] = m
        stl[2 * NEIGH], str_[2 * NEIGH] = m[OWN - RIM_S :], m[:RIM_S]
        for k in range(NEIGH):
            g = w[k] * m
            position = lax.broadcasted_iota(jnp.int32, (OWN, LANES), 1) + off[k]
            lane[k, own] = position & (LANES - 1)
            step[k, own] = position >> 7
            gain[k, own] = g
            f = off[k].astype(jnp.float32)
            stl[k], str_[k] = f[OWN - RIM_S :], f[:RIM_S]
            stl[NEIGH + k], str_[NEIGH + k] = g[OWN - RIM_S :], g[:RIM_S]
        stat = [
            remote(stl, rstl, s_stat.at[0], r_stat.at[0], after, inst),
            remote(str_, rstr, s_stat.at[1], r_stat.at[1], before, inst),
        ]

        @pl.when(has_after)
        def _():
            stat[0].start()

        @pl.when(has_before)
        def _():
            stat[1].start()

        ro[inst] = sx[mine]

        @pl.when(has_before)
        def _():
            stat[0].wait_recv()

        @pl.when(first)
        def _():
            rl[...] = jnp.zeros_like(rl)
            rstl[...] = jnp.zeros_like(rstl)

        @pl.when(has_after)
        def _():
            stat[1].wait_recv()

        @pl.when(last)
        def _():
            rr[...] = jnp.zeros_like(rr)
            rstr[...] = jnp.zeros_like(rstr)

        for start, got in ((RIM - RIM_S, rstl), (RIM + OWN, rstr)):
            rows = pl.ds(start, RIM_S)
            for k in range(NEIGH):
                position = lax.broadcasted_iota(jnp.int32, (RIM_S, LANES), 1) + got[k].astype(jnp.int32)
                lane[k, rows] = position & (LANES - 1)
                step[k, rows] = position >> 7
                gain[k, rows] = got[NEIGH + k]
            scale[rows] = got[2 * NEIGH]

        def transform(read, rows, dst, to):
            h = forward([read(n) for n in range(NI)])
            for j in range(NI):
                dst[j, pl.ds(to, rows)] = h[j]

        def rim(ref, which, row, rows):
            base = (0, PER * RIM)[which] + row
            size = (RIM, RIM_S)[which]
            return lambda n: ref[n // PER, pl.ds(base + (n % PER) * size, rows)]

        def all_of(ref, sem):
            pltpu.make_async_copy(ref, ref, sem).wait()

        @pl.when(has_before)
        def _():
            all_of(rl, r_left)

        transform(rim(rl, 0, 0, 2), 2, even, 0)
        transform(rim(rl, 0, 2, 8), 8, even, 2)
        transform(rim(rl, 1, 0, 8), 8, src, 2)

        @pl.when(has_after)
        def _():
            all_of(rr, r_right)

        transform(rim(rr, 0, 8, 2), 2, even, RIM + OWN + 8)
        transform(rim(rr, 0, 0, 8), 8, even, RIM + OWN)
        transform(rim(rr, 1, 0, 8), 8, src, RIM + OWN)
        all_of(ro.at[pl.ds(1, GROUP - 1)], r_own)
        for t in range(0, OWN, 8):
            for which, dst in ((0, even), (1, src)):
                transform(lambda n: ro[n // PER, which, n % PER, pl.ds(t, 8)], 8, dst, RIM + t)

        def sweep(old, new, start, to, harmonics):
            rows = pl.ds(start, 8)
            m = scale[rows]
            names = [j for k in harmonics for j in ((2 * k - 1, 2 * k) if 0 < k < 8 else (max(2 * k - 1, 0),))]
            total = {}
            for k in harmonics:
                if k in (0, 8):
                    j = max(2 * k - 1, 0)
                    total[j] = (1.0 - RELAX) * old[j, rows] + m * src[j, rows]
                else:
                    a, b = 2 * k - 1, 2 * k
                    xa, xb = old[a, rows], old[b, rows]
                    total[a] = (1.0 - RELAX) * xa + m * (src[a, rows] - (FREQ * k) * xb)
                    total[b] = (1.0 - RELAX) * xb + m * (src[b, rows] + (FREQ * k) * xa)
            for k in range(NEIGH):
                sign = 1 if k % 2 else -1
                index, by, g = lane[k, rows], step[k, rows], gain[k, rows]
                near, next_ = by == 0, by == sign
                for j in names:
                    pick = [
                        jnp.take_along_axis(old[j, pl.ds(start + sign * d, 8)], index, axis=1, mode="promise_in_bounds")
                        for d in range(REACH + 1)
                    ]
                    total[j] = total[j] + g * jnp.where(near, pick[0], jnp.where(next_, pick[1], pick[2]))
            for j in names:
                new[j, pl.ds(to, 8)] = total[j]

        low, high = (0, 1), tuple(range(2, 9))
        buffers = (even, odd)
        for harmonics, sweeps in ((low, SWEEPS), (high, SWEEPS_FINE)):
            for s in range(sweeps):
                wide = (sweeps - 1 - s) * REACH
                old, new = buffers[s % 2], buffers[(s + 1) % 2]
                for start in tiles(RIM - wide, RIM + OWN + wide):
                    if s < sweeps - 1:
                        sweep(old, new, start, start, harmonics)
                    else:
                        sweep(old, fin, start, start - RIM, harmonics)
        for t in range(0, OWN, 8):
            rows = pl.ds(t, 8)
            x = backward([fin[j, rows] for j in range(NI)])
            for n in range(NI):
                back[n // PER, n % PER, rows] = x[n]
        home = [remote(back.at[i], out.at[:, mine], s_out, r_out, cell, i) for i in range(GROUP)]
        for i in range(GROUP):

            @pl.when(inst != i)
            def _():
                home[i].start()

        out[:, mine] = back[inst]
        all_of(back.at[pl.ds(1, GROUP - 1)], s_out)

        @pl.when(has_after)
        def _():
            stat[0].wait_send()

        @pl.when(has_before)
        def _():
            stat[1].wait_send()

        all_of(sx.at[pl.ds(1, COMP - 1)], s_own)
        all_of(out.at[:, pl.ds(1, COMP - 1)], r_out)

    @pl.when(idle)
    def _():
        for copy in load[2:]:
            copy.wait()
        pltpu.make_async_copy(sx, sx, s_own).wait()
        pltpu.make_async_copy(out, out, r_out).wait()

    @pl.when(has_after)
    def _():
        pltpu.make_async_copy(sl, sl, s_left).wait()

    @pl.when(has_before)
    def _():
        pltpu.make_async_copy(sr, sr, s_right).wait()


def per_device(initial, source, neighbors, face_weights, damping):
    vmem = pl.BlockSpec(memory_space=pltpu.VMEM)
    f32, i32 = jnp.float32, jnp.int32
    dma = pltpu.SemaphoreType.DMA
    arguments = (initial, source, neighbors, face_weights, damping.reshape(OWN, LANES))
    result = pl.pallas_call(
        kernel,
        out_shape=pltpu.VMEM((PER, COMP, OWN, LANES), f32),
        in_specs=[pl.BlockSpec(memory_space=pltpu.HBM)] * 5,
        out_specs=vmem,
        scratch_shapes=[
            pltpu.VMEM((PER * COMP, OWN * LANES), f32),
            pltpu.VMEM((PER * COMP, OWN * LANES), f32),
            pltpu.VMEM((NEIGH, OWN * LANES), i32),
            pltpu.VMEM((NEIGH, OWN * LANES), f32),
            pltpu.VMEM((OWN, LANES), f32),
            pltpu.VMEM((COMP, 2, PER, OWN, LANES), f32),
            pltpu.VMEM((COMP, MESSAGE, LANES), f32),
            pltpu.VMEM((COMP, MESSAGE, LANES), f32),
            pltpu.VMEM((2 * NEIGH + 1, RIM_S, LANES), f32),
            pltpu.VMEM((2 * NEIGH + 1, RIM_S, LANES), f32),
            pltpu.VMEM((GROUP, 2, PER, OWN, LANES), f32),
            pltpu.VMEM((GROUP, MESSAGE, LANES), f32),
            pltpu.VMEM((GROUP, MESSAGE, LANES), f32),
            pltpu.VMEM((2 * NEIGH + 1, RIM_S, LANES), f32),
            pltpu.VMEM((2 * NEIGH + 1, RIM_S, LANES), f32),
            pltpu.VMEM((NEIGH, ROWS, LANES), i32),
            pltpu.VMEM((NEIGH, ROWS, LANES), i32),
            pltpu.VMEM((NEIGH, ROWS, LANES), f32),
            pltpu.VMEM((ROWS, LANES), f32),
            pltpu.VMEM((NI, ROWS, LANES), f32),
            pltpu.VMEM((NI, ROWS, LANES), f32),
            pltpu.VMEM((NI, ROWS, LANES), f32),
            pltpu.VMEM((NI, OWN, LANES), f32),
            pltpu.VMEM((GROUP, PER, OWN, LANES), f32),
            dma((5,)), dma, dma, dma, dma((2,)), dma, dma, dma, dma((2,)), dma, dma,
        ],
        compiler_params=pltpu.CompilerParams(
            collective_id=0, has_side_effects=True, vmem_limit_bytes=32 * 1024 * 1024
        ),
    )(*(pltpu.with_memory_space_constraint(x, pltpu.HBM) for x in arguments))
    return result.reshape(PER * COMP, OWN * LANES)


def solution(mesh):
    return jax.shard_map(
        per_device,
        mesh=mesh,
        in_specs=(
            P("inst", "cell"),
            P("inst", "cell"),
            P(None, "cell"),
            P(None, "cell"),
            P("cell"),
        ),
        out_specs=P("inst", "cell"),
        check_vma=False,
    )
```

time: 28.5 us -> 23.8 us (0.84)
  Pallas kernels: 26.7 us -> 23 us
  local copies, waits for them, and re-layouts: 1.6 us -> 0.71 us
    pallas_call x1, Pallas kernels: 26.7 us -> 23 us  [per_device(): pl.pallas_call(kernel, out_shape=pltpu.VMEM((PER, COMP, OWN, LANES), f32)...]
    unnamed x2, local copies, waits for them, and re-layouts: 1.6 us -> 0.71 us
where the time goes in v3:
time: 23.8 us; the launch traced here: 23.7 us
  Pallas kernels  23 us (97%)
  local copies, waits for them, and re-layouts  0.71 us (3%)
    pallas_call x1, Pallas kernels, per_device(): pl.pallas_call(kernel, out_shape=pltpu.VMEM((PER, COMP, OWN, LANES), f32)...  23 us
    unnamed x2, local copies, waits for them, and re-layouts  0.71 us

profile of v3, /device:TPU:1, one launch (start us, length us, event | category | flops | bytes accessed | tf_op | source)
XLA Modules:
  0.0 23.7 jit_solution(4700687409763096155)
XLA Ops:
  0.0 23.0 %shard_map.55 = f32[2,5,16,128]{3,2,1,0:T(8,128)S(1)} custom-call(f32[10,2048]{1,0:T(8,128)} %initial_in.1, f32[10,2048]{1,0:T(8,128)} %source_in.1, s32[4,2048]{1,0:T(4,128)} %neighbors_in.1, f32[4,2048]{1,0:T(4,128)} %weights_in.1, f32[16,128]{1,0:T(8,128)} %bitcast.7), custom_call_target="tpu_custom_call" | custom-call | tf_op jit(solution)/shard_map/pallas_call | solution.py:350
  23.0 0.7 %copy.6 = f32[2,8,16,128]{3,1,2,0:T(8,128)} copy(f32[2,8,16,128]{3,2,1,0:T(8,128)S(1)} %bitcast.6) | data formatting | bytes 262144
  (1 shorter events, 0.0 us)

commit v4 on v3

--- a/solution.py
+++ b/solution.py
@@ -22,8 +22,10 @@
 ROWS = OWN + 2 * RIM
 GROUP = 8
 PER = NI // GROUP
-MESSAGE = PER * (RIM + RIM_S) + 4
-OWNERS = (0, 1, 2, 4, 6)
+NEAR = SWEEPS_FINE * REACH
+FAR, FAR_S = RIM - NEAR, RIM_S - NEAR
+M_NEAR, M_FAR = 16, 24
+OWNERS = ((1, 2, 4, 5, 6), (0, 1, 3, 6, 7))
 MESH = pl.DeviceIdType.MESH
 ROOT = math.sqrt(0.5)
 
@@ -53,6 +55,16 @@
     return out
 
 
+def forward_low(x):
+    p = [x[n] + x[n + 8] for n in range(8)]
+    q = [x[n] - x[n + 8] for n in range(8)]
+    a, b = q[0] * 0.125, q[4] * 0.125
+    for n in (1, 2, 3):
+        a = a + (q[n] - q[8 - n]) * (math.cos(math.pi * n / 8) / 8)
+        b = b + (q[n] + q[8 - n]) * (math.sin(math.pi * n / 8) / 8)
+    return [(((p[0] + p[4]) + (p[2] + p[6])) + ((p[1] + p[5]) + (p[3] + p[7]))) * 0.0625, a, b]
+
+
 def backward(h):
     a = {k: h[2 * k - 1] for k in range(1, 9)}
     a[0] = h[0]
@@ -81,9 +93,9 @@
 def kernel(
     initial_in, source_in, neighbors_in, weights_in, damping_in, out,
     initial, source, neighbors, weights, damping,
-    sx, sl, sr, stl, str_, ro, rl, rr, rstl, rstr,
+    sx, sl, sr, fl, fr, stl, str_, ro, rl, rr, gl, gr, rstl, rstr,
     lane, step, gain, scale, even, odd, src, fin, back,
-    s_in, s_own, s_left, s_right, s_stat, r_own, r_left, r_right, r_stat, s_out, r_out,
+    s_in, s_own, s_left, s_right, s_fl, s_fr, s_stat, r_own, r_left, r_right, r_fl, r_fr, r_stat, s_out, r_out,
 ):
     cell, inst = lax.axis_index("cell"), lax.axis_index("inst")
     count = lax.axis_size("cell")
@@ -91,10 +103,14 @@
     has_before, has_after = jnp.logical_not(first), jnp.logical_not(last)
     after, before = jnp.minimum(cell + 1, count - 1), jnp.maximum(cell - 1, 0)
     sides = has_before.astype(jnp.int32) + has_after.astype(jnp.int32)
-    mine, owns = 0, 0
+    parity = lax.rem(cell, 2)
+    here = [OWNERS[0][v] + parity * (OWNERS[1][v] - OWNERS[0][v]) for v in range(COMP)]
+    beside = [OWNERS[1][v] + parity * (OWNERS[0][v] - OWNERS[1][v]) for v in range(COMP)]
+    mine, owns, serves = 0, 0, 0
     for v in range(COMP):
-        here = (inst == OWNERS[v]).astype(jnp.int32)
-        mine, owns = mine + v * here, owns + here
+        hit = (inst == here[v]).astype(jnp.int32)
+        mine, owns = mine + v * hit, owns + hit
+        serves = serves + (inst == beside[v]).astype(jnp.int32)
     busy = owns == 1
     idle = jnp.logical_not(busy)
 
@@ -130,16 +146,38 @@
         for j in range(1, GROUP):
             greet(cell, lax.rem(inst + j, GROUP))
 
+    for copy in load[2:]:
+        copy.wait()
+    w = [weights[pl.ds(k, 1), :].reshape(OWN, LANES) for k in range(NEIGH)]
+    off = [neighbors[pl.ds(k, 1), :].reshape(OWN, LANES) for k in range(NEIGH)]
+    m = RELAX / (damping[...] + ((w[0] + w[1]) + (w[2] + w[3])))
+    own = pl.ds(RIM, OWN)
+    scale[own] = m
+    stl[2 * NEIGH], str_[2 * NEIGH] = m[OWN - RIM_S :], m[:RIM_S]
+    for k in range(NEIGH):
+        g = w[k] * m
+        position = lax.broadcasted_iota(jnp.int32, (OWN, LANES), 1) + off[k]
+        lane[k, own] = position & (LANES - 1)
+        step[k, own] = position >> 7
+        gain[k, own] = g
+        f = off[k].astype(jnp.float32)
+        stl[k], str_[k] = f[OWN - RIM_S :], f[:RIM_S]
+        stl[NEIGH + k], str_[NEIGH + k] = g[OWN - RIM_S :], g[:RIM_S]
+
+    pad = jnp.zeros((COMP, M_FAR - PER * (FAR + FAR_S), LANES), jnp.float32)
+    fl[:, PER * (FAR + FAR_S) :], fr[:, PER * (FAR + FAR_S) :] = pad, pad
+
     for which, ref in enumerate((initial, source)):
         load[which].wait()
         for n in range(PER):
             for v in range(COMP):
                 x = ref[pl.ds(n * COMP + v, 1), :].reshape(OWN, LANES)
                 sx[v, which, n] = x
-                size = (RIM, RIM_S)[which]
-                rows = pl.ds((n * RIM, PER * RIM + n * RIM_S)[which], size)
-                sl[v, rows] = x[OWN - size :]
-                sr[v, rows] = x[:size]
+                rows = pl.ds((which * PER + n) * NEAR, NEAR)
+                sl[v, rows], sr[v, rows] = x[OWN - NEAR :], x[:NEAR]
+                size = (FAR, FAR_S)[which]
+                rows = pl.ds((n * FAR, PER * FAR + n * FAR_S)[which], size)
+                fl[v, rows], fr[v, rows] = x[OWN - NEAR - size : OWN - NEAR], x[NEAR : NEAR + size]
 
     pl.semaphore_wait(barrier, COMP * (1 + sides) - owns)
 
@@ -148,9 +186,16 @@
             src_ref=a, dst_ref=b, send_sem=s, recv_sem=r, device_id={"cell": c, "inst": i}, device_id_type=MESH
         )
 
-    own_copy = [remote(sx.at[v], ro.at[inst], s_own, r_own, cell, OWNERS[v]) for v in range(COMP)]
-    left_copy = [remote(sl.at[v], rl.at[inst], s_left, r_left, after, OWNERS[v]) for v in range(COMP)]
-    right_copy = [remote(sr.at[v], rr.at[inst], s_right, r_right, before, OWNERS[v]) for v in range(COMP)]
+    own_copy = [remote(sx.at[v], ro.at[inst], s_own, r_own, cell, here[v]) for v in range(COMP)]
+    left_copy = [remote(sl.at[v], rl.at[inst], s_left, r_left, after, beside[v]) for v in range(COMP)]
+    right_copy = [remote(sr.at[v], rr.at[inst], s_right, r_right, before, beside[v]) for v in range(COMP)]
+    far_left_copy = [remote(fl.at[v], gl.at[inst], s_fl, r_fl, after, beside[v]) for v in range(COMP)]
+    far_right_copy = [remote(fr.at[v], gr.at[inst], s_fr, r_fr, before, beside[v]) for v in range(COMP)]
+    stat = [
+        remote(stl, rstl, s_stat.at[0], r_stat.at[0], after, inst),
+        remote(str_, rstr, s_stat.at[1], r_stat.at[1], before, inst),
+    ]
+    give = [jnp.logical_and(has_after, serves == 1), jnp.logical_and(has_before, serves == 1)]
 
     for v in range(COMP):
 
@@ -168,56 +213,44 @@
         for v in range(COMP):
             right_copy[v].start()
 
+    for side in range(2):
+
+        @pl.when(give[side])
+        def _():
+            stat[side].start()
+
+    @pl.when(has_after)
+    def _():
+        for v in range(COMP):
+            far_left_copy[v].start()
+
+    @pl.when(has_before)
+    def _():
+        for v in range(COMP):
+            far_right_copy[v].start()
+
     @pl.when(busy)
     def _():
-        for copy in load[2:]:
-            copy.wait()
-        w = [weights[pl.ds(k, 1), :].reshape(OWN, LANES) for k in range(NEIGH)]
-        off = [neighbors[pl.ds(k, 1), :].reshape(OWN, LANES) for k in range(NEIGH)]
-        m = RELAX / (damping[...] + ((w[0] + w[1]) + (w[2] + w[3])))
-        own = pl.ds(RIM, OWN)
-        scale[own] = m
-        stl[2 * NEIGH], str_[2 * NEIGH] = m[OWN - RIM_S :], m[:RIM_S]
-        for k in range(NEIGH):
-            g = w[k] * m
-            position = lax.broadcasted_iota(jnp.int32, (OWN, LANES), 1) + off[k]
-            lane[k, own] = position & (LANES - 1)
-            step[k, own] = position >> 7
-            gain[k, own] = g
-            f = off[k].astype(jnp.float32)
-            stl[k], str_[k] = f[OWN - RIM_S :], f[:RIM_S]
-            stl[NEIGH + k], str_[NEIGH + k] = g[OWN - RIM_S :], g[:RIM_S]
-        stat = [
-            remote(stl, rstl, s_stat.at[0], r_stat.at[0], after, inst),
-            remote(str_, rstr, s_stat.at[1], r_stat.at[1], before, inst),
-        ]
+        ro[inst] = sx[mine]
+
+        @pl.when(has_before)
+        def _():
+            stat[0].wait_recv()
+
+        @pl.when(first)
+        def _():
+            rl[...] = jnp.zeros_like(rl)
+            gl[...] = jnp.zeros_like(gl)
+            rstl[...] = jnp.zeros_like(rstl)
 
         @pl.when(has_after)
         def _():
-            stat[0].start()
-
-        @pl.when(has_before)
-        def _():
-            stat[1].start()
-
-        ro[inst] = sx[mine]
-
-        @pl.when(has_before)
-        def _():
-            stat[0].wait_recv()
-
-        @pl.when(first)
-        def _():
-            rl[...] = jnp.zeros_like(rl)
-            rstl[...] = jnp.zeros_like(rstl)
-
-        @pl.when(has_after)
-        def _():
             stat[1].wait_recv()
 
         @pl.when(last)
         def _():
             rr[...] = jnp.zeros_like(rr)
+            gr[...] = jnp.zeros_like(gr)
             rstr[...] = jnp.zeros_like(rstr)
 
         for start, got in ((RIM - RIM_S, rstl), (RIM + OWN, rstr)):
@@ -229,38 +262,37 @@
                 gain[k, rows] = got[NEIGH + k]
             scale[rows] = got[2 * NEIGH]
 
-        def transform(read, rows, dst, to):
-            h = forward([read(n) for n in range(NI)])
-            for j in range(NI):
+        def transform(read, rows, dst, to, change=forward):
+            h = change([read(n) for n in range(NI)])
+            for j in range(len(h)):
                 dst[j, pl.ds(to, rows)] = h[j]
 
-        def rim(ref, which, row, rows):
-            base = (0, PER * RIM)[which] + row
-            size = (RIM, RIM_S)[which]
-            return lambda n: ref[n // PER, pl.ds(base + (n % PER) * size, rows)]
+        def near(ref, which):
+            return lambda n: ref[n // PER, pl.ds((which * PER + n % PER) * NEAR, NEAR)]
+
+        def far(ref, which):
+            base, size = (0, PER * FAR)[which], (FAR, FAR_S)[which]
+            return lambda n: ref[n // PER, pl.ds(base + (n % PER) * size, size)]
 
         def all_of(ref, sem):
             pltpu.make_async_copy(ref, ref, sem).wait()
 
-        @pl.when(has_before)
-        def _():
-            all_of(rl, r_left)
-
-        transform(rim(rl, 0, 0, 2), 2, even, 0)
-        transform(rim(rl, 0, 2, 8), 8, even, 2)
-        transform(rim(rl, 1, 0, 8), 8, src, 2)
-
-        @pl.when(has_after)
-        def _():
-            all_of(rr, r_right)
-
-        transform(rim(rr, 0, 8, 2), 2, even, RIM + OWN + 8)
-        transform(rim(rr, 0, 0, 8), 8, even, RIM + OWN)
-        transform(rim(rr, 1, 0, 8), 8, src, RIM + OWN)
         all_of(ro.at[pl.ds(1, GROUP - 1)], r_own)
         for t in range(0, OWN, 8):
             for which, dst in ((0, even), (1, src)):
                 transform(lambda n: ro[n // PER, which, n % PER, pl.ds(t, 8)], 8, dst, RIM + t)
+
+        @pl.when(has_before)
+        def _():
+            all_of(rl, r_left)
+
+        @pl.when(has_after)
+        def _():
+            all_of(rr, r_right)
+
+        for which, dst in ((0, even), (1, src)):
+            transform(near(rl, which), NEAR, dst, RIM - NEAR)
+            transform(near(rr, which), NEAR, dst, RIM + OWN)
 
         def sweep(old, new, start, to, harmonics):
             rows = pl.ds(start, 8)
@@ -291,7 +323,7 @@
 
         low, high = (0, 1), tuple(range(2, 9))
         buffers = (even, odd)
-        for harmonics, sweeps in ((low, SWEEPS), (high, SWEEPS_FINE)):
+        def relax(harmonics, sweeps):
             for s in range(sweeps):
                 wide = (sweeps - 1 - s) * REACH
                 old, new = buffers[s % 2], buffers[(s + 1) % 2]
@@ -300,6 +332,22 @@
                         sweep(old, new, start, start, harmonics)
                     else:
                         sweep(old, fin, start, start - RIM, harmonics)
+
+        relax(high, SWEEPS_FINE)
+
+        @pl.when(has_before)
+        def _():
+            all_of(gl, r_fl)
+
+        @pl.when(has_after)
+        def _():
+            all_of(gr, r_fr)
+
+        transform(far(gl, 0), FAR, even, 0, forward_low)
+        transform(far(gl, 1), FAR_S, src, RIM - RIM_S, forward_low)
+        transform(far(gr, 0), FAR, even, RIM + OWN + NEAR, forward_low)
+        transform(far(gr, 1), FAR_S, src, RIM + OWN + NEAR, forward_low)
+        relax(low, SWEEPS)
         for t in range(0, OWN, 8):
             rows = pl.ds(t, 8)
             x = backward([fin[j, rows] for j in range(NI)])
@@ -315,31 +363,29 @@
         out[:, mine] = back[inst]
         all_of(back.at[pl.ds(1, GROUP - 1)], s_out)
 
-        @pl.when(has_after)
-        def _():
-            stat[0].wait_send()
-
-        @pl.when(has_before)
-        def _():
-            stat[1].wait_send()
-
         all_of(sx.at[pl.ds(1, COMP - 1)], s_own)
         all_of(out.at[:, pl.ds(1, COMP - 1)], r_out)
 
     @pl.when(idle)
     def _():
-        for copy in load[2:]:
-            copy.wait()
         pltpu.make_async_copy(sx, sx, s_own).wait()
         pltpu.make_async_copy(out, out, r_out).wait()
 
+    for side in range(2):
+
+        @pl.when(give[side])
+        def _():
+            stat[side].wait_send()
+
     @pl.when(has_after)
     def _():
         pltpu.make_async_copy(sl, sl, s_left).wait()
+        pltpu.make_async_copy(fl, fl, s_fl).wait()
 
     @pl.when(has_before)
     def _():
         pltpu.make_async_copy(sr, sr, s_right).wait()
+        pltpu.make_async_copy(fr, fr, s_fr).wait()
 
 
 def per_device(initial, source, neighbors, face_weights, damping):
@@ -359,13 +405,17 @@
             pltpu.VMEM((NEIGH, OWN * LANES), f32),
             pltpu.VMEM((OWN, LANES), f32),
             pltpu.VMEM((COMP, 2, PER, OWN, LANES), f32),
-            pltpu.VMEM((COMP, MESSAGE, LANES), f32),
-            pltpu.VMEM((COMP, MESSAGE, LANES), f32),
+            pltpu.VMEM((COMP, M_NEAR, LANES), f32),
+            pltpu.VMEM((COMP, M_NEAR, LANES), f32),
+            pltpu.VMEM((COMP, M_FAR, LANES), f32),
+            pltpu.VMEM((COMP, M_FAR, LANES), f32),
             pltpu.VMEM((2 * NEIGH + 1, RIM_S, LANES), f32),
             pltpu.VMEM((2 * NEIGH + 1, RIM_S, LANES), f32),
             pltpu.VMEM((GROUP, 2, PER, OWN, LANES), f32),
-            pltpu.VMEM((GROUP, MESSAGE, LANES), f32),
-            pltpu.VMEM((GROUP, MESSAGE, LANES), f32),
+            pltpu.VMEM((GROUP, M_NEAR, LANES), f32),
+            pltpu.VMEM((GROUP, M_NEAR, LANES), f32),
+            pltpu.VMEM((GROUP, M_FAR, LANES), f32),
+            pltpu.VMEM((GROUP, M_FAR, LANES), f32),
             pltpu.VMEM((2 * NEIGH + 1, RIM_S, LANES), f32),
             pltpu.VMEM((2 * NEIGH + 1, RIM_S, LANES), f32),
             pltpu.VMEM((NEIGH, ROWS, LANES), i32),
@@ -377,7 +427,7 @@
             pltpu.VMEM((NI, ROWS, LANES), f32),
             pltpu.VMEM((NI, OWN, LANES), f32),
             pltpu.VMEM((GROUP, PER, OWN, LANES), f32),
-            dma((5,)), dma, dma, dma, dma((2,)), dma, dma, dma, dma((2,)), dma, dma,
+            dma((5,)), dma, dma, dma, dma, dma, dma((2,)), dma, dma, dma, dma, dma, dma((2,)), dma, dma,
         ],
         compiler_params=pltpu.CompilerParams(
             collective_id=0, has_side_effects=True, vmem_limit_bytes=32 * 1024 * 1024

time: 23.8 us -> 22.1 us (0.929)
  Pallas kernels: 23 us -> 21.3 us
    pallas_call x1, Pallas kernels: 23 us -> 21.3 us  [per_device(): pl.pallas_call(kernel, out_shape=pltpu.VMEM((PER, COMP, OWN, LANES), f32)...]
where the time goes in v4:
time: 22.1 us; the launch traced here: 22 us
  Pallas kernels  21.3 us (96%)
  local copies, waits for them, and re-layouts  0.71 us (3%)
    pallas_call x1, Pallas kernels, per_device(): pl.pallas_call(kernel, out_shape=pltpu.VMEM((PER, COMP, OWN, LANES), f32)...  21.3 us
    unnamed x2, local copies, waits for them, and re-layouts  0.71 us

profile of v4, /device:TPU:1, one launch (start us, length us, event | category | flops | bytes accessed | tf_op | source)
XLA Modules:
  0.0 22.0 jit_solution(16753311746269020640)
XLA Ops:
  0.0 21.3 %shard_map.55 = f32[2,5,16,128]{3,2,1,0:T(8,128)S(1)} custom-call(f32[10,2048]{1,0:T(8,128)} %initial_in.1, f32[10,2048]{1,0:T(8,128)} %source_in.1, s32[4,2048]{1,0:T(4,128)} %neighbors_in.1, f32[4,2048]{1,0:T(4,128)} %weights_in.1, f32[16,128]{1,0:T(8,128)} %bitcast.7), custom_call_target="tpu_custom_call" | custom-call | tf_op jit(solution)/shard_map/pallas_call | solution.py:396
  21.3 0.7 %copy.6 = f32[2,8,16,128]{3,1,2,0:T(8,128)} copy(f32[2,8,16,128]{3,2,1,0:T(8,128)S(1)} %bitcast.6) | data formatting | bytes 262144
  (1 shorter events, 0.0 us)

commit v5 on v4

--- a/solution.py
+++ b/solution.py
@@ -24,8 +24,9 @@
 PER = NI // GROUP
 NEAR = SWEEPS_FINE * REACH
 FAR, FAR_S = RIM - NEAR, RIM_S - NEAR
-M_NEAR, M_FAR = 16, 24
-OWNERS = ((1, 2, 4, 5, 6), (0, 1, 3, 6, 7))
+LOW = 3
+M_NEAR, M_FAR = 16, PER * (FAR + FAR_S)
+OWNERS = ((1, 2, 3, 4, 5), (0, 1, 4, 6, 7))
 MESH = pl.DeviceIdType.MESH
 ROOT = math.sqrt(0.5)
 
@@ -93,26 +94,32 @@
 def kernel(
     initial_in, source_in, neighbors_in, weights_in, damping_in, out,
     initial, source, neighbors, weights, damping,
-    sx, sl, sr, fl, fr, stl, str_, ro, rl, rr, gl, gr, rstl, rstr,
+    sx, sn, sf, st_outer, st_flip, ro, rn, rf, got_outer, got_flip, hs, hr,
     lane, step, gain, scale, even, odd, src, fin, back,
-    s_in, s_own, s_left, s_right, s_fl, s_fr, s_stat, r_own, r_left, r_right, r_fl, r_fr, r_stat, s_out, r_out,
+    s_in, s_own, s_near, s_far, s_stat, s_rim, r_own, r_near, r_far, r_stat, r_rim, s_out, r_out,
 ):
     cell, inst = lax.axis_index("cell"), lax.axis_index("inst")
     count = lax.axis_size("cell")
-    first, last = cell == 0, cell == count - 1
-    has_before, has_after = jnp.logical_not(first), jnp.logical_not(last)
-    after, before = jnp.minimum(cell + 1, count - 1), jnp.maximum(cell - 1, 0)
-    sides = has_before.astype(jnp.int32) + has_after.astype(jnp.int32)
-    parity = lax.rem(cell, 2)
-    here = [OWNERS[0][v] + parity * (OWNERS[1][v] - OWNERS[0][v]) for v in range(COMP)]
-    beside = [OWNERS[1][v] + parity * (OWNERS[0][v] - OWNERS[1][v]) for v in range(COMP)]
+    odd_block = lax.rem(cell, 2)
+    is_even = odd_block == 0
+    flip = cell + 1 - 2 * odd_block
+    beyond = cell - 1 + 2 * odd_block
+    has_outer = jnp.logical_and(beyond >= 0, beyond < count)
+    outer = jnp.minimum(jnp.maximum(beyond, 0), count - 1)
+
+    def owners(c):
+        high = lax.rem(lax.div(c, 2), 2)
+        return [OWNERS[0][v] + high * (OWNERS[1][v] - OWNERS[0][v]) for v in range(COMP)]
+
+    here, there = owners(cell), owners(cell + 2)
     mine, owns, serves = 0, 0, 0
     for v in range(COMP):
         hit = (inst == here[v]).astype(jnp.int32)
         mine, owns = mine + v * hit, owns + hit
-        serves = serves + (inst == beside[v]).astype(jnp.int32)
+        serves = serves + (inst == there[v]).astype(jnp.int32)
     busy = owns == 1
     idle = jnp.logical_not(busy)
+    give = jnp.logical_and(has_outer, serves == 1)
 
     load = [
         pltpu.make_async_copy(a, b, s_in.at[j])
@@ -136,13 +143,12 @@
 
     @pl.when(busy)
     def _():
-        for has, c in ((has_before, before), (has_after, after)):
-
-            @pl.when(has)
-            def _():
-                for i in range(GROUP):
-                    greet(c, i)
-
+        @pl.when(has_outer)
+        def _():
+            for i in range(GROUP):
+                greet(outer, i)
+
+        greet(flip, inst)
         for j in range(1, GROUP):
             greet(cell, lax.rem(inst + j, GROUP))
 
@@ -153,19 +159,22 @@
     m = RELAX / (damping[...] + ((w[0] + w[1]) + (w[2] + w[3])))
     own = pl.ds(RIM, OWN)
     scale[own] = m
-    stl[2 * NEIGH], str_[2 * NEIGH] = m[OWN - RIM_S :], m[:RIM_S]
+
+    def edges(k, x):
+        head, tail = x[:RIM_S], x[OWN - RIM_S :]
+        st_outer[k], st_flip[k] = jnp.where(is_even, head, tail), jnp.where(is_even, tail, head)
+
+    edges(2 * NEIGH, m)
     for k in range(NEIGH):
         g = w[k] * m
         position = lax.broadcasted_iota(jnp.int32, (OWN, LANES), 1) + off[k]
         lane[k, own] = position & (LANES - 1)
         step[k, own] = position >> 7
         gain[k, own] = g
-        f = off[k].astype(jnp.float32)
-        stl[k], str_[k] = f[OWN - RIM_S :], f[:RIM_S]
-        stl[NEIGH + k], str_[NEIGH + k] = g[OWN - RIM_S :], g[:RIM_S]
-
-    pad = jnp.zeros((COMP, M_FAR - PER * (FAR + FAR_S), LANES), jnp.float32)
-    fl[:, PER * (FAR + FAR_S) :], fr[:, PER * (FAR + FAR_S) :] = pad, pad
+        edges(k, off[k].astype(jnp.float32))
+        edges(NEIGH + k, g)
+
+    hs[NI:] = jnp.zeros((2 * LOW, 8, LANES), jnp.float32)
 
     for which, ref in enumerate((initial, source)):
         load[which].wait()
@@ -173,13 +182,13 @@
             for v in range(COMP):
                 x = ref[pl.ds(n * COMP + v, 1), :].reshape(OWN, LANES)
                 sx[v, which, n] = x
-                rows = pl.ds((which * PER + n) * NEAR, NEAR)
-                sl[v, rows], sr[v, rows] = x[OWN - NEAR :], x[:NEAR]
+                near_rows = pl.ds((which * PER + n) * NEAR, NEAR)
+                sn[v, near_rows] = jnp.where(is_even, x[:NEAR], x[OWN - NEAR :])
                 size = (FAR, FAR_S)[which]
-                rows = pl.ds((n * FAR, PER * FAR + n * FAR_S)[which], size)
-                fl[v, rows], fr[v, rows] = x[OWN - NEAR - size : OWN - NEAR], x[NEAR : NEAR + size]
-
-    pl.semaphore_wait(barrier, COMP * (1 + sides) - owns)
+                far_rows = pl.ds((n * FAR, PER * FAR + n * FAR_S)[which], size)
+                sf[v, far_rows] = jnp.where(is_even, x[NEAR : NEAR + size], x[OWN - NEAR - size : OWN - NEAR])
+
+    pl.semaphore_wait(barrier, COMP * (1 + has_outer.astype(jnp.int32)))
 
     def remote(a, b, s, r, c, i):
         return pltpu.make_async_remote_copy(
@@ -187,15 +196,11 @@
         )
 
     own_copy = [remote(sx.at[v], ro.at[inst], s_own, r_own, cell, here[v]) for v in range(COMP)]
-    left_copy = [remote(sl.at[v], rl.at[inst], s_left, r_left, after, beside[v]) for v in range(COMP)]
-    right_copy = [remote(sr.at[v], rr.at[inst], s_right, r_right, before, beside[v]) for v in range(COMP)]
-    far_left_copy = [remote(fl.at[v], gl.at[inst], s_fl, r_fl, after, beside[v]) for v in range(COMP)]
-    far_right_copy = [remote(fr.at[v], gr.at[inst], s_fr, r_fr, before, beside[v]) for v in range(COMP)]
-    stat = [
-        remote(stl, rstl, s_stat.at[0], r_stat.at[0], after, inst),
-        remote(str_, rstr, s_stat.at[1], r_stat.at[1], before, inst),
-    ]
-    give = [jnp.logical_and(has_after, serves == 1), jnp.logical_and(has_before, serves == 1)]
+    near_copy = [remote(sn.at[v], rn.at[inst], s_near, r_near, outer, there[v]) for v in range(COMP)]
+    far_copy = [remote(sf.at[v], rf.at[inst], s_far, r_far, outer, there[v]) for v in range(COMP)]
+    stat_outer = remote(st_outer, got_outer, s_stat.at[0], r_stat.at[0], outer, inst)
+    stat_flip = remote(st_flip, got_flip, s_stat.at[1], r_stat.at[1], flip, inst)
+    rim_flip = remote(hs, hr, s_rim, r_rim, flip, inst)
 
     for v in range(COMP):
 
@@ -203,57 +208,47 @@
         def _():
             own_copy[v].start()
 
-    @pl.when(has_after)
+    @pl.when(has_outer)
     def _():
         for v in range(COMP):
-            left_copy[v].start()
-
-    @pl.when(has_before)
+            near_copy[v].start()
+
+    @pl.when(give)
+    def _():
+        stat_outer.start()
+
+    @pl.when(has_outer)
     def _():
         for v in range(COMP):
-            right_copy[v].start()
-
-    for side in range(2):
-
-        @pl.when(give[side])
-        def _():
-            stat[side].start()
-
-    @pl.when(has_after)
-    def _():
-        for v in range(COMP):
-            far_left_copy[v].start()
-
-    @pl.when(has_before)
-    def _():
-        for v in range(COMP):
-            far_right_copy[v].start()
+            far_copy[v].start()
 
     @pl.when(busy)
     def _():
+        stat_flip.start()
         ro[inst] = sx[mine]
 
-        @pl.when(has_before)
-        def _():
-            stat[0].wait_recv()
-
-        @pl.when(first)
-        def _():
-            rl[...] = jnp.zeros_like(rl)
-            gl[...] = jnp.zeros_like(gl)
-            rstl[...] = jnp.zeros_like(rstl)
-
-        @pl.when(has_after)
-        def _():
-            stat[1].wait_recv()
-
-        @pl.when(last)
-        def _():
-            rr[...] = jnp.zeros_like(rr)
-            gr[...] = jnp.zeros_like(gr)
-            rstr[...] = jnp.zeros_like(rstr)
-
-        for start, got in ((RIM - RIM_S, rstl), (RIM + OWN, rstr)):
+        @pl.when(has_outer)
+        def _():
+            stat_outer.wait_recv()
+
+        @pl.when(jnp.logical_not(has_outer))
+        def _():
+            rn[...] = jnp.zeros_like(rn)
+            rf[...] = jnp.zeros_like(rf)
+            got_outer[...] = jnp.zeros_like(got_outer)
+
+        stat_flip.wait_recv()
+
+        def pick(even_row, odd_row):
+            return even_row + odd_block * (odd_row - even_row)
+
+        left, right = (RIM - NEAR, 0, FAR - FAR_S), (RIM + OWN, RIM + OWN + NEAR, RIM + OWN + NEAR)
+        at_outer = [pick(a, b) for a, b in zip(left, right)]
+        at_flip = [pick(b, a) for a, b in zip(left, right)]
+        for start, got in (
+            (pick(RIM - RIM_S, RIM + OWN), got_outer),
+            (pick(RIM + OWN, RIM - RIM_S), got_flip),
+        ):
             rows = pl.ds(start, RIM_S)
             for k in range(NEIGH):
                 position = lax.broadcasted_iota(jnp.int32, (RIM_S, LANES), 1) + got[k].astype(jnp.int32)
@@ -282,17 +277,26 @@
             for which, dst in ((0, even), (1, src)):
                 transform(lambda n: ro[n // PER, which, n % PER, pl.ds(t, 8)], 8, dst, RIM + t)
 
-        @pl.when(has_before)
-        def _():
-            all_of(rl, r_left)
-
-        @pl.when(has_after)
-        def _():
-            all_of(rr, r_right)
+        to_near, to_far, to_far_s = pick(RIM + OWN - NEAR, RIM), pick(RIM + OWN - RIM, RIM + NEAR), pick(RIM + OWN - RIM_S, RIM + NEAR)
+        for j in range(NI):
+            hs[j, :NEAR], hs[j, NEAR:] = even[j, pl.ds(to_near, NEAR)], src[j, pl.ds(to_near, NEAR)]
+        for j in range(LOW):
+            hs[NI + j, :FAR] = even[j, pl.ds(to_far, FAR)]
+            hs[NI + LOW + j, :FAR_S] = src[j, pl.ds(to_far_s, FAR_S)]
+        rim_flip.start()
+
+        @pl.when(has_outer)
+        def _():
+            all_of(rn, r_near)
 
         for which, dst in ((0, even), (1, src)):
-            transform(near(rl, which), NEAR, dst, RIM - NEAR)
-            transform(near(rr, which), NEAR, dst, RIM + OWN)
+            transform(near(rn, which), NEAR, dst, at_outer[0])
+        rim_flip.wait_recv()
+        for j in range(NI):
+            even[j, pl.ds(at_flip[0], NEAR)], src[j, pl.ds(at_flip[0], NEAR)] = hr[j, :NEAR], hr[j, NEAR:]
+        for j in range(LOW):
+            even[j, pl.ds(at_flip[1], FAR)] = hr[NI + j, :FAR]
+            src[j, pl.ds(at_flip[2], FAR_S)] = hr[NI + LOW + j, :FAR_S]
 
         def sweep(old, new, start, to, harmonics):
             rows = pl.ds(start, 8)
@@ -335,18 +339,12 @@
 
         relax(high, SWEEPS_FINE)
 
-        @pl.when(has_before)
-        def _():
-            all_of(gl, r_fl)
-
-        @pl.when(has_after)
-        def _():
-            all_of(gr, r_fr)
-
-        transform(far(gl, 0), FAR, even, 0, forward_low)
-        transform(far(gl, 1), FAR_S, src, RIM - RIM_S, forward_low)
-        transform(far(gr, 0), FAR, even, RIM + OWN + NEAR, forward_low)
-        transform(far(gr, 1), FAR_S, src, RIM + OWN + NEAR, forward_low)
+        @pl.when(has_outer)
+        def _():
+            all_of(rf, r_far)
+
+        transform(far(rf, 0), FAR, even, at_outer[1], forward_low)
+        transform(far(rf, 1), FAR_S, src, at_outer[2], forward_low)
         relax(low, SWEEPS)
         for t in range(0, OWN, 8):
             rows = pl.ds(t, 8)
@@ -364,6 +362,8 @@
         all_of(back.at[pl.ds(1, GROUP - 1)], s_out)
 
         all_of(sx.at[pl.ds(1, COMP - 1)], s_own)
+        stat_flip.wait_send()
+        rim_flip.wait_send()
         all_of(out.at[:, pl.ds(1, COMP - 1)], r_out)
 
     @pl.when(idle)
@@ -371,21 +371,14 @@
         pltpu.make_async_copy(sx, sx, s_own).wait()
         pltpu.make_async_copy(out, out, r_out).wait()
 
-    for side in range(2):
-
-        @pl.when(give[side])
-        def _():
-            stat[side].wait_send()
-
-    @pl.when(has_after)
-    def _():
-        pltpu.make_async_copy(sl, sl, s_left).wait()
-        pltpu.make_async_copy(fl, fl, s_fl).wait()
-
-    @pl.when(has_before)
-    def _():
-        pltpu.make_async_copy(sr, sr, s_right).wait()
-        pltpu.make_async_copy(fr, fr, s_fr).wait()
+    @pl.when(give)
+    def _():
+        stat_outer.wait_send()
+
+    @pl.when(has_outer)
+    def _():
+        pltpu.make_async_copy(sn, sn, s_near).wait()
+        pltpu.make_async_copy(sf, sf, s_far).wait()
 
 
 def per_device(initial, source, neighbors, face_weights, damping):
@@ -406,18 +399,16 @@
             pltpu.VMEM((OWN, LANES), f32),
             pltpu.VMEM((COMP, 2, PER, OWN, LANES), f32),
             pltpu.VMEM((COMP, M_NEAR, LANES), f32),
-            pltpu.VMEM((COMP, M_NEAR, LANES), f32),
-            pltpu.VMEM((COMP, M_FAR, LANES), f32),
             pltpu.VMEM((COMP, M_FAR, LANES), f32),
             pltpu.VMEM((2 * NEIGH + 1, RIM_S, LANES), f32),
             pltpu.VMEM((2 * NEIGH + 1, RIM_S, LANES), f32),
             pltpu.VMEM((GROUP, 2, PER, OWN, LANES), f32),
             pltpu.VMEM((GROUP, M_NEAR, LANES), f32),
-            pltpu.VMEM((GROUP, M_NEAR, LANES), f32),
-            pltpu.VMEM((GROUP, M_FAR, LANES), f32),
             pltpu.VMEM((GROUP, M_FAR, LANES), f32),
             pltpu.VMEM((2 * NEIGH + 1, RIM_S, LANES), f32),
             pltpu.VMEM((2 * NEIGH + 1, RIM_S, LANES), f32),
+            pltpu.VMEM((NI + 2 * LOW, 8, LANES), f32),
+            pltpu.VMEM((NI + 2 * LOW, 8, LANES), f32),
             pltpu.VMEM((NEIGH, ROWS, LANES), i32),
             pltpu.VMEM((NEIGH, ROWS, LANES), i32),
             pltpu.VMEM((NEIGH, ROWS, LANES), f32),
@@ -427,7 +418,7 @@
             pltpu.VMEM((NI, ROWS, LANES), f32),
             pltpu.VMEM((NI, OWN, LANES), f32),
             pltpu.VMEM((GROUP, PER, OWN, LANES), f32),
-            dma((5,)), dma, dma, dma, dma, dma, dma((2,)), dma, dma, dma, dma, dma, dma((2,)), dma, dma,
+            dma((5,)), dma, dma, dma, dma((2,)), dma, dma, dma, dma, dma((2,)), dma, dma, dma,
         ],
         compiler_params=pltpu.CompilerParams(
             collective_id=0, has_side_effects=True, vmem_limit_bytes=32 * 1024 * 1024

time: 22.1 us -> 22.9 us (1.036)
  Pallas kernels: 21.3 us -> 22.1 us
    pallas_call x1, Pallas kernels: 21.3 us -> 22.1 us  [per_device(): pl.pallas_call(kernel, out_shape=pltpu.VMEM((PER, COMP, OWN, LANES), f32)...]
where the time goes in v5:
time: 22.9 us; the launch traced here: 22.8 us
  Pallas kernels  22.1 us (97%)
  local copies, waits for them, and re-layouts  0.71 us (3%)
    pallas_call x1, Pallas kernels, per_device(): pl.pallas_call(kernel, out_shape=pltpu.VMEM((PER, COMP, OWN, LANES), f32)...  22.1 us
    unnamed x2, local copies, waits for them, and re-layouts  0.71 us

profile of v5, /device:TPU:1, one launch (start us, length us, event | category | flops | bytes accessed | tf_op | source)
XLA Modules:
  0.0 22.8 jit_solution(18393737838275803769)
XLA Ops:
  0.0 22.1 %shard_map.55 = f32[2,5,16,128]{3,2,1,0:T(8,128)S(1)} custom-call(f32[10,2048]{1,0:T(8,128)} %initial_in.1, f32[10,2048]{1,0:T(8,128)} %source_in.1, s32[4,2048]{1,0:T(4,128)} %neighbors_in.1, f32[4,2048]{1,0:T(4,128)} %weights_in.1, f32[16,128]{1,0:T(8,128)} %bitcast.7), custom_call_target="tpu_custom_call" | custom-call | tf_op jit(solution)/shard_map/pallas_call | solution.py:389
  22.1 0.7 %copy.6 = f32[2,8,16,128]{3,1,2,0:T(8,128)} copy(f32[2,8,16,128]{3,2,1,0:T(8,128)S(1)} %bitcast.6) | data formatting | bytes 262144
  (1 shorter events, 0.0 us)

commit v6 on v5

--- a/solution.py
+++ b/solution.py
@@ -26,7 +26,7 @@
 FAR, FAR_S = RIM - NEAR, RIM_S - NEAR
 LOW = 3
 M_NEAR, M_FAR = 16, PER * (FAR + FAR_S)
-OWNERS = ((1, 2, 3, 4, 5), (0, 1, 4, 6, 7))
+OWNERS = ((1, 2, 3, 4, 6), (0, 1, 2, 4, 6))
 MESH = pl.DeviceIdType.MESH
 ROOT = math.sqrt(0.5)
 

time: 22.9 us -> 21 us (0.917)
  Pallas kernels: 22.1 us -> 20.1 us
    pallas_call x1, Pallas kernels: 22.1 us -> 20.1 us  [per_device(): pl.pallas_call(kernel, out_shape=pltpu.VMEM((PER, COMP, OWN, LANES), f32)...]
where the time goes in v6:
time: 21 us; the launch traced here: 20.8 us
  Pallas kernels  20.1 us (96%)
  local copies, waits for them, and re-layouts  0.71 us (3%)
    pallas_call x1, Pallas kernels, per_device(): pl.pallas_call(kernel, out_shape=pltpu.VMEM((PER, COMP, OWN, LANES), f32)...  20.1 us
    unnamed x2, local copies, waits for them, and re-layouts  0.71 us

profile of v6, /device:TPU:1, one launch (start us, length us, event | category | flops | bytes accessed | tf_op | source)
XLA Modules:
  0.0 20.8 jit_solution(16916314452466300431)
XLA Ops:
  0.0 20.1 %shard_map.55 = f32[2,5,16,128]{3,2,1,0:T(8,128)S(1)} custom-call(f32[10,2048]{1,0:T(8,128)} %initial_in.1, f32[10,2048]{1,0:T(8,128)} %source_in.1, s32[4,2048]{1,0:T(4,128)} %neighbors_in.1, f32[4,2048]{1,0:T(4,128)} %weights_in.1, f32[16,128]{1,0:T(8,128)} %bitcast.7), custom_call_target="tpu_custom_call" | custom-call | tf_op jit(solution)/shard_map/pallas_call | solution.py:389
  20.1 0.7 %copy.6 = f32[2,8,16,128]{3,1,2,0:T(8,128)} copy(f32[2,8,16,128]{3,2,1,0:T(8,128)S(1)} %bitcast.6) | data formatting | bytes 262144
  (1 shorter events, 0.0 us)

commit v7 on v6

--- a/solution.py
+++ b/solution.py
@@ -271,32 +271,6 @@
 
         def all_of(ref, sem):
             pltpu.make_async_copy(ref, ref, sem).wait()
-
-        all_of(ro.at[pl.ds(1, GROUP - 1)], r_own)
-        for t in range(0, OWN, 8):
-            for which, dst in ((0, even), (1, src)):
-                transform(lambda n: ro[n // PER, which, n % PER, pl.ds(t, 8)], 8, dst, RIM + t)
-
-        to_near, to_far, to_far_s = pick(RIM + OWN - NEAR, RIM), pick(RIM + OWN - RIM, RIM + NEAR), pick(RIM + OWN - RIM_S, RIM + NEAR)
-        for j in range(NI):
-            hs[j, :NEAR], hs[j, NEAR:] = even[j, pl.ds(to_near, NEAR)], src[j, pl.ds(to_near, NEAR)]
-        for j in range(LOW):
-            hs[NI + j, :FAR] = even[j, pl.ds(to_far, FAR)]
-            hs[NI + LOW + j, :FAR_S] = src[j, pl.ds(to_far_s, FAR_S)]
-        rim_flip.start()
-
-        @pl.when(has_outer)
-        def _():
-            all_of(rn, r_near)
-
-        for which, dst in ((0, even), (1, src)):
-            transform(near(rn, which), NEAR, dst, at_outer[0])
-        rim_flip.wait_recv()
-        for j in range(NI):
-            even[j, pl.ds(at_flip[0], NEAR)], src[j, pl.ds(at_flip[0], NEAR)] = hr[j, :NEAR], hr[j, NEAR:]
-        for j in range(LOW):
-            even[j, pl.ds(at_flip[1], FAR)] = hr[NI + j, :FAR]
-            src[j, pl.ds(at_flip[2], FAR_S)] = hr[NI + LOW + j, :FAR_S]
 
         def sweep(old, new, start, to, harmonics):
             rows = pl.ds(start, 8)
@@ -327,8 +301,8 @@
 
         low, high = (0, 1), tuple(range(2, 9))
         buffers = (even, odd)
-        def relax(harmonics, sweeps):
-            for s in range(sweeps):
+        def relax(harmonics, sweeps, first=0):
+            for s in range(first, sweeps):
                 wide = (sweeps - 1 - s) * REACH
                 old, new = buffers[s % 2], buffers[(s + 1) % 2]
                 for start in tiles(RIM - wide, RIM + OWN + wide):
@@ -337,7 +311,39 @@
                     else:
                         sweep(old, fin, start, start - RIM, harmonics)
 
-        relax(high, SWEEPS_FINE)
+        all_of(ro.at[pl.ds(1, GROUP - 1)], r_own)
+        for t in range(0, OWN, 8):
+            for which, dst in ((0, even), (1, src)):
+                transform(lambda n: ro[n // PER, which, n % PER, pl.ds(t, 8)], 8, dst, RIM + t)
+
+        to_near, to_far, to_far_s = pick(RIM + OWN - NEAR, RIM), pick(RIM + OWN - RIM, RIM + NEAR), pick(RIM + OWN - RIM_S, RIM + NEAR)
+        for j in range(NI):
+            hs[j, :NEAR], hs[j, NEAR:] = even[j, pl.ds(to_near, NEAR)], src[j, pl.ds(to_near, NEAR)]
+        for j in range(LOW):
+            hs[NI + j, :FAR] = even[j, pl.ds(to_far, FAR)]
+            hs[NI + LOW + j, :FAR_S] = src[j, pl.ds(to_far_s, FAR_S)]
+        rim_flip.start()
+        ends = (RIM - REACH, RIM + OWN + REACH - 8)
+        sweep(even, odd, RIM + 6, RIM + 6, high)
+
+        @pl.when(has_outer)
+        def _():
+            all_of(rn, r_near)
+
+        for which, dst in ((0, even), (1, src)):
+            transform(near(rn, which), NEAR, dst, at_outer[0])
+        start = pick(*ends)
+        sweep(even, odd, start, start, high)
+        rim_flip.wait_recv()
+        for j in range(NI):
+            even[j, pl.ds(at_flip[0], NEAR)], src[j, pl.ds(at_flip[0], NEAR)] = hr[j, :NEAR], hr[j, NEAR:]
+        for j in range(LOW):
+            even[j, pl.ds(at_flip[1], FAR)] = hr[NI + j, :FAR]
+            src[j, pl.ds(at_flip[2], FAR_S)] = hr[NI + LOW + j, :FAR_S]
+
+        start = pick(*ends[::-1])
+        sweep(even, odd, start, start, high)
+        relax(high, SWEEPS_FINE, 1)
 
         @pl.when(has_outer)
         def _():

time: 21 us -> 20.7 us (0.986)
  Pallas kernels: 20.1 us -> 19.8 us
    pallas_call x1, Pallas kernels: 20.1 us -> 19.8 us  [per_device(): pl.pallas_call(kernel, out_shape=pltpu.VMEM((PER, COMP, OWN, LANES), f32)...]
where the time goes in v7:
time: 20.7 us; the launch traced here: 20.6 us
  Pallas kernels  19.8 us (96%)
  local copies, waits for them, and re-layouts  0.71 us (3%)
    pallas_call x1, Pallas kernels, per_device(): pl.pallas_call(kernel, out_shape=pltpu.VMEM((PER, COMP, OWN, LANES), f32)...  19.8 us
    unnamed x2, local copies, waits for them, and re-layouts  0.71 us

profile of v7, /device:TPU:1, one launch (start us, length us, event | category | flops | bytes accessed | tf_op | source)
XLA Modules:
  0.0 20.6 jit_solution(315705258617205440)
XLA Ops:
  0.0 19.8 %shard_map.55 = f32[2,5,16,128]{3,2,1,0:T(8,128)S(1)} custom-call(f32[10,2048]{1,0:T(8,128)} %initial_in.1, f32[10,2048]{1,0:T(8,128)} %source_in.1, s32[4,2048]{1,0:T(4,128)} %neighbors_in.1, f32[4,2048]{1,0:T(4,128)} %weights_in.1, f32[16,128]{1,0:T(8,128)} %bitcast.7), custom_call_target="tpu_custom_call" | custom-call | tf_op jit(solution)/shard_map/pallas_call | solution.py:395
  19.9 0.7 %copy.6 = f32[2,8,16,128]{3,1,2,0:T(8,128)} copy(f32[2,8,16,128]{3,2,1,0:T(8,128)S(1)} %bitcast.6) | data formatting | bytes 262144
  (1 shorter events, 0.0 us)

commit v8 on v7

--- a/solution.py
+++ b/solution.py
@@ -121,6 +121,16 @@
     idle = jnp.logical_not(busy)
     give = jnp.logical_and(has_outer, serves == 1)
 
+    barrier = pltpu.get_barrier_semaphore()
+
+    def greet(c, i):
+        pl.semaphore_signal(barrier, inc=1, device_id={"cell": c, "inst": i}, device_id_type=MESH)
+
+    @pl.when(busy)
+    def _():
+        for j in range(1, GROUP):
+            greet(cell, lax.rem(inst + j, GROUP))
+
     load = [
         pltpu.make_async_copy(a, b, s_in.at[j])
         for j, (a, b) in enumerate(
@@ -136,11 +146,6 @@
     for copy in load:
         copy.start()
 
-    barrier = pltpu.get_barrier_semaphore()
-
-    def greet(c, i):
-        pl.semaphore_signal(barrier, inc=1, device_id={"cell": c, "inst": i}, device_id_type=MESH)
-
     @pl.when(busy)
     def _():
         @pl.when(has_outer)
@@ -149,8 +154,6 @@
                 greet(outer, i)
 
         greet(flip, inst)
-        for j in range(1, GROUP):
-            greet(cell, lax.rem(inst + j, GROUP))
 
     for copy in load[2:]:
         copy.wait()
@@ -301,15 +304,14 @@
 
         low, high = (0, 1), tuple(range(2, 9))
         buffers = (even, odd)
-        def relax(harmonics, sweeps, first=0):
-            for s in range(first, sweeps):
-                wide = (sweeps - 1 - s) * REACH
-                old, new = buffers[s % 2], buffers[(s + 1) % 2]
-                for start in tiles(RIM - wide, RIM + OWN + wide):
-                    if s < sweeps - 1:
-                        sweep(old, new, start, start, harmonics)
-                    else:
-                        sweep(old, fin, start, start - RIM, harmonics)
+        def relax(harmonics, sweeps, s):
+            wide = (sweeps - 1 - s) * REACH
+            old, new = buffers[s % 2], buffers[(s + 1) % 2]
+            for start in tiles(RIM - wide, RIM + OWN + wide):
+                if s < sweeps - 1:
+                    sweep(old, new, start, start, harmonics)
+                else:
+                    sweep(old, fin, start, start - RIM, harmonics)
 
         all_of(ro.at[pl.ds(1, GROUP - 1)], r_own)
         for t in range(0, OWN, 8):
@@ -343,7 +345,6 @@
 
         start = pick(*ends[::-1])
         sweep(even, odd, start, start, high)
-        relax(high, SWEEPS_FINE, 1)
 
         @pl.when(has_outer)
         def _():
@@ -351,14 +352,17 @@
 
         transform(far(rf, 0), FAR, even, at_outer[1], forward_low)
         transform(far(rf, 1), FAR_S, src, at_outer[2], forward_low)
-        relax(low, SWEEPS)
+        for s in range(SWEEPS):
+            relax(low, SWEEPS, s)
+            if s < OWN // 8:
+                sweep(odd, fin, RIM + 8 * s, 8 * s, high)
         for t in range(0, OWN, 8):
             rows = pl.ds(t, 8)
             x = backward([fin[j, rows] for j in range(NI)])
             for n in range(NI):
                 back[n // PER, n % PER, rows] = x[n]
         home = [remote(back.at[i], out.at[:, mine], s_out, r_out, cell, i) for i in range(GROUP)]
-        for i in range(GROUP):
+        for i in (0, 2, 6, 4, 1, 3, 7, 5):
 
             @pl.when(inst != i)
             def _():

time: 20.7 us -> 20.6 us (level); the launches traced: 20.6 us -> 20.2 us
  Pallas kernels: 19.8 us -> 19.5 us
    pallas_call x1, Pallas kernels: 19.8 us -> 19.5 us  [per_device(): pl.pallas_call(kernel, out_shape=pltpu.VMEM((PER, COMP, OWN, LANES), f32)...]
where the time goes in v8:
time: 20.6 us; the launch traced here: 20.2 us
  Pallas kernels  19.5 us (95%)
  local copies, waits for them, and re-layouts  0.71 us (3%)
    pallas_call x1, Pallas kernels, per_device(): pl.pallas_call(kernel, out_shape=pltpu.VMEM((PER, COMP, OWN, LANES), f32)...  19.5 us
    unnamed x2, local copies, waits for them, and re-layouts  0.71 us

profile of v8, /device:TPU:1, one launch (start us, length us, event | category | flops | bytes accessed | tf_op | source)
XLA Modules:
  0.0 20.2 jit_solution(9044630190537181228)
XLA Ops:
  0.0 19.5 %shard_map.55 = f32[2,5,16,128]{3,2,1,0:T(8,128)S(1)} custom-call(f32[10,2048]{1,0:T(8,128)} %initial_in.1, f32[10,2048]{1,0:T(8,128)} %source_in.1, s32[4,2048]{1,0:T(4,128)} %neighbors_in.1, f32[4,2048]{1,0:T(4,128)} %weights_in.1, f32[16,128]{1,0:T(8,128)} %bitcast.7), custom_call_target="tpu_custom_call" | custom-call | tf_op jit(solution)/shard_map/pallas_call | solution.py:399
  19.5 0.7 %copy.6 = f32[2,8,16,128]{3,1,2,0:T(8,128)} copy(f32[2,8,16,128]{3,2,1,0:T(8,128)S(1)} %bitcast.6) | data formatting | bytes 262144
  (1 shorter events, 0.0 us)

commit v9 on v8

--- a/solution.py
+++ b/solution.py
@@ -155,30 +155,6 @@
 
         greet(flip, inst)
 
-    for copy in load[2:]:
-        copy.wait()
-    w = [weights[pl.ds(k, 1), :].reshape(OWN, LANES) for k in range(NEIGH)]
-    off = [neighbors[pl.ds(k, 1), :].reshape(OWN, LANES) for k in range(NEIGH)]
-    m = RELAX / (damping[...] + ((w[0] + w[1]) + (w[2] + w[3])))
-    own = pl.ds(RIM, OWN)
-    scale[own] = m
-
-    def edges(k, x):
-        head, tail = x[:RIM_S], x[OWN - RIM_S :]
-        st_outer[k], st_flip[k] = jnp.where(is_even, head, tail), jnp.where(is_even, tail, head)
-
-    edges(2 * NEIGH, m)
-    for k in range(NEIGH):
-        g = w[k] * m
-        position = lax.broadcasted_iota(jnp.int32, (OWN, LANES), 1) + off[k]
-        lane[k, own] = position & (LANES - 1)
-        step[k, own] = position >> 7
-        gain[k, own] = g
-        edges(k, off[k].astype(jnp.float32))
-        edges(NEIGH + k, g)
-
-    hs[NI:] = jnp.zeros((2 * LOW, 8, LANES), jnp.float32)
-
     for which, ref in enumerate((initial, source)):
         load[which].wait()
         for n in range(PER):
@@ -216,6 +192,28 @@
         for v in range(COMP):
             near_copy[v].start()
 
+    for copy in load[2:]:
+        copy.wait()
+    w = [weights[pl.ds(k, 1), :].reshape(OWN, LANES) for k in range(NEIGH)]
+    off = [neighbors[pl.ds(k, 1), :].reshape(OWN, LANES) for k in range(NEIGH)]
+    m = RELAX / (damping[...] + ((w[0] + w[1]) + (w[2] + w[3])))
+    own = pl.ds(RIM, OWN)
+    scale[own] = m
+
+    def edges(k, x):
+        head, tail = x[:RIM_S], x[OWN - RIM_S :]
+        st_outer[k], st_flip[k] = jnp.where(is_even, head, tail), jnp.where(is_even, tail, head)
+
+    edges(2 * NEIGH, m)
+    for k in range(NEIGH):
+        g = w[k] * m
+        position = lax.broadcasted_iota(jnp.int32, (OWN, LANES), 1) + off[k]
+        lane[k, own] = position & (LANES - 1)
+        step[k, own] = position >> 7
+        gain[k, own] = g
+        edges(k, off[k].astype(jnp.float32))
+        edges(NEIGH + k, g)
+
     @pl.when(give)
     def _():
         stat_outer.start()
@@ -224,6 +222,8 @@
     def _():
         for v in range(COMP):
             far_copy[v].start()
+
+    hs[NI:] = jnp.zeros((2 * LOW, 8, LANES), jnp.float32)
 
     @pl.when(busy)
     def _():

time: 20.6 us -> 20.6 us (level)
  no operation moved by 1% of the time
where the time goes in v9:
time: 20.6 us; the launch traced here: 20.2 us
  Pallas kernels  19.5 us (95%)
  local copies, waits for them, and re-layouts  0.71 us (3%)
    pallas_call x1, Pallas kernels, per_device(): pl.pallas_call(kernel, out_shape=pltpu.VMEM((PER, COMP, OWN, LANES), f32)...  19.5 us
    unnamed x2, local copies, waits for them, and re-layouts  0.71 us

profile of v9, /device:TPU:1, one launch (start us, length us, event | category | flops | bytes accessed | tf_op | source)
XLA Modules:
  0.0 20.2 jit_solution(6159996071085076904)
XLA Ops:
  0.0 19.5 %shard_map.55 = f32[2,5,16,128]{3,2,1,0:T(8,128)S(1)} custom-call(f32[10,2048]{1,0:T(8,128)} %initial_in.1, f32[10,2048]{1,0:T(8,128)} %source_in.1, s32[4,2048]{1,0:T(4,128)} %neighbors_in.1, f32[4,2048]{1,0:T(4,128)} %weights_in.1, f32[16,128]{1,0:T(8,128)} %bitcast.7), custom_call_target="tpu_custom_call" | custom-call | tf_op jit(solution)/shard_map/pallas_call | solution.py:399
  19.5 0.7 %copy.6 = f32[2,8,16,128]{3,1,2,0:T(8,128)} copy(f32[2,8,16,128]{3,2,1,0:T(8,128)S(1)} %bitcast.6) | data formatting | bytes 262144
  (1 shorter events, 0.0 us)

commit v10 on v8

--- a/solution.py
+++ b/solution.py
@@ -346,16 +346,21 @@
         start = pick(*ends[::-1])
         sweep(even, odd, start, start, high)
 
+        for t in range(0, OWN, 8):
+            sweep(even, odd, RIM + t, RIM + t, low)
+        sweep(odd, fin, RIM, 0, high)
+
         @pl.when(has_outer)
         def _():
             all_of(rf, r_far)
 
         transform(far(rf, 0), FAR, even, at_outer[1], forward_low)
         transform(far(rf, 1), FAR_S, src, at_outer[2], forward_low)
-        for s in range(SWEEPS):
+        for start in (RIM - RIM_S, RIM + OWN):
+            sweep(even, odd, start, start, low)
+        sweep(odd, fin, RIM + 8, 8, high)
+        for s in range(1, SWEEPS):
             relax(low, SWEEPS, s)
-            if s < OWN // 8:
-                sweep(odd, fin, RIM + 8 * s, 8 * s, high)
         for t in range(0, OWN, 8):
             rows = pl.ds(t, 8)
             x = backward([fin[j, rows] for j in range(NI)])

time: 20.6 us -> 20.6 us (level)
  no operation moved by 1% of the time
where the time goes in v10:
time: 20.6 us; the launch traced here: 20.2 us
  Pallas kernels  19.5 us (95%)
  local copies, waits for them, and re-layouts  0.71 us (3%)
    pallas_call x1, Pallas kernels, per_device(): pl.pallas_call(kernel, out_shape=pltpu.VMEM((PER, COMP, OWN, LANES), f32)...  19.5 us
    unnamed x2, local copies, waits for them, and re-layouts  0.71 us

profile of v10, /device:TPU:1, one launch (start us, length us, event | category | flops | bytes accessed | tf_op | source)
XLA Modules:
  0.0 20.2 jit_solution(6766413727535644093)
XLA Ops:
  0.0 19.5 %shard_map.55 = f32[2,5,16,128]{3,2,1,0:T(8,128)S(1)} custom-call(f32[10,2048]{1,0:T(8,128)} %initial_in.1, f32[10,2048]{1,0:T(8,128)} %source_in.1, s32[4,2048]{1,0:T(4,128)} %neighbors_in.1, f32[4,2048]{1,0:T(4,128)} %weights_in.1, f32[16,128]{1,0:T(8,128)} %bitcast.7), custom_call_target="tpu_custom_call" | custom-call | tf_op jit(solution)/shard_map/pallas_call | solution.py:404
  19.6 0.7 %copy.6 = f32[2,8,16,128]{3,1,2,0:T(8,128)} copy(f32[2,8,16,128]{3,2,1,0:T(8,128)S(1)} %bitcast.6) | data formatting | bytes 262144
  (1 shorter events, 0.0 us)
